TPU v7x, 128 devices: a whole 4x4x4 slice. The times are simulated.
128 devices in a mesh: rotor: 8 (over y, core), stator: 16 (over x, z).
Axes of the slice: x: 4, y: 4, z: 4, core: 2. Of those that a mesh axis runs over, the one named last changes fastest.
Arguments:
- rotor_state: float32 [5, 8, 8, 8, 49152], P(None, None, None, None, ('rotor', 'stator')), as said below
- stator_state: float32 [5, 8, 8, 8, 49152], P(None, None, None, None, ('rotor', 'stator')), as said below
- rotor_projection: float32 [2, 64, 64], replicated, as said below
- proj_stator: float32 [2, 64, 64], replicated, as said below
- seg_owner: int32 [98304, 1], P(('rotor', 'stator')), may hold values from 0 to 127; in each aligned block of 768 rows (0 to 767, 768 to 1535, ...) at most 12 rows name the same one
- seg_row: int32 [98304], P(('rotor', 'stator')), may hold values from 0 to 383
Outputs:
- rotor_next: float32 [5, 8, 8, 8, 49152], P(None, None, None, None, ('rotor', 'stator'))
- stator_next: float32 [5, 8, 8, 8, 49152], P(None, None, None, None, ('rotor', 'stator'))
Inputs may be any that keep to these rules, and one draw needn't show every extreme that they name: `seg_owner`: in each aligned block of 768 rows (the segments of one band device) no owner is named by more than 12 rows, a bound that some block reaches. `rotor_state`: density is positive at every node, and so is 0.4 (energy - |momentum|^2 / (2 density)). `stator_state`: density is positive at every node, and so is 0.4 (energy - |momentum|^2 / (2 density)). `rotor_projection`: entries are non-negative. `proj_stator`: entries are non-negative.
All inputs are finite; a program needn't handle non-finite values.
Results may differ from a plain program's by a relative error of at most 0.0001.
Values sent between devices are 32-bit elements; how exact they have to be, the bound alone decides.
A program may use at most 192 MiB of HBM per device.

v0:
```python
import jax
import jax.numpy as jnp
import numpy as np
from jax import lax
from jax.sharding import PartitionSpec as P

NODES = 8


GAMMA = 1.4
TIME_STEP = 0.02
LIFT_FACTOR = 28.0
TOP_PRECISION = lax.Precision.HIGHEST


def cheb_matrix():
    degree = NODES - 1
    j = np.arange(degree + 1)
    points = -np.cos(np.pi * j / degree)
    weights = np.where((j == 0) | (j == degree), 2.0, 1.0) * (-1.0) ** j
    spacing = points[:, None] - points[None, :]
    identity = np.eye(degree + 1)
    matrix = weights[:, None] / weights[None, :] / (spacing + identity)
    matrix = matrix - identity * matrix.sum(axis=1)[:, None]
    return matrix.astype(np.float32)


def primitive(fields):
    density, momentum_x, momentum_y, momentum_z, energy = fields
    inverse = 1.0 / density
    velocity = (momentum_x * inverse, momentum_y * inverse, momentum_z * inverse)
    kinetic = momentum_x * velocity[0] + momentum_y * velocity[1] + momentum_z * velocity[2]
    pressure = (GAMMA - 1.0) * (energy - 0.5 * kinetic)
    return (velocity, pressure)


def directional_flux(fields, velocity, pressure, direction):
    normal_speed = velocity[direction]
    result = [fields[1 + direction]]
    for component in range(3):
        product = fields[1 + component] * normal_speed
        if component == direction:
            product = product + pressure
        result.append(product)
    result.append((fields[4] + pressure) * normal_speed)
    return result


def rusanov_leading(rotor_side, stator_side):
    left_fields = [rotor_side[variable] for variable in range(5)]
    right_fields = [stator_side[variable] for variable in range(5)]
    left_velocity, left_pressure = primitive(left_fields)
    right_velocity, right_pressure = primitive(right_fields)
    left_flux = directional_flux(left_fields, left_velocity, left_pressure, 2)
    right_flux = directional_flux(right_fields, right_velocity, right_pressure, 2)
    signal = jnp.maximum(
        jnp.abs(left_velocity[2]) + jnp.sqrt(GAMMA * left_pressure / left_fields[0]),
        jnp.abs(right_velocity[2]) + jnp.sqrt(GAMMA * right_pressure / right_fields[0]),
    )
    merged = [
        0.5 * (left_flux[variable] + right_flux[variable])
        - 0.5 * signal * (right_fields[variable] - left_fields[variable])
        for variable in range(5)
    ]
    return jnp.stack(merged, axis=0)


def volume_rate(conserved, matrix):
    fields = [conserved[variable] for variable in range(5)]
    velocity, pressure = primitive(fields)
    patterns = ("ij,vjbce->vibce", "ij,vajce->vaice", "ij,vabje->vabie")
    divergence = jnp.zeros_like(conserved)
    for direction in range(3):
        flux_values = jnp.stack(directional_flux(fields, velocity, pressure, direction))
        divergence = divergence + jnp.einsum(
            patterns[direction], matrix, flux_values, precision=TOP_PRECISION
        )
    return -divergence


def face_flux(face_state):
    fields = [face_state[variable] for variable in range(5)]
    velocity, pressure = primitive(fields)
    return jnp.stack(directional_flux(fields, velocity, pressure, 2))


def body(rotor_state, stator_state, rotor_projection, proj_stator, seg_owner, seg_row):
    matrix = jnp.asarray(cheb_matrix())
    elements = rotor_state.shape[-1]
    surface_nodes = NODES * NODES
    row_width = 5 * surface_nodes
    rotors = lax.axis_size("rotor")
    devices = lax.axis_size(("rotor", "stator"))
    capacity = max(2, 4 * elements // devices)
    slot_count = devices * capacity
    segments = 2 * elements
    band_rows = elements // rotors
    rotor_trace = rotor_state[:, :, :, NODES - 1, :].reshape(5, surface_nodes, elements)
    projected = jnp.einsum("sij,vjf->visf", rotor_projection, rotor_trace, precision=TOP_PRECISION)
    moved = lax.all_to_all(
        projected.reshape(5, surface_nodes, 2, rotors, band_rows),
        "rotor",
        split_axis=3,
        concat_axis=3,
        tiled=True,
    )
    rotor_side = moved.reshape(row_width, segments)
    stator_faces = stator_state[:, :, :, 0, :].reshape(5, surface_nodes, elements)
    owners = seg_owner[:, 0].reshape(elements, 2).T.reshape(segments)
    rows_side = seg_row.reshape(elements, 2).T.reshape(segments)
    side_bit = jnp.arange(segments, dtype=jnp.int32) // elements
    onehot = (owners[:, None] == jnp.arange(devices, dtype=jnp.int32)[None, :]).astype(jnp.int32)
    earlier = jnp.cumsum(onehot, axis=0) - onehot
    position = owners * capacity + jnp.sum(earlier * onehot, axis=1)
    outgoing_codes = (
        jnp.full((slot_count,), -1, jnp.int32)
        .at[position]
        .set(rows_side * 2 + side_bit)
        .reshape(1, 1, slot_count)
    )
    outgoing_values = (
        jnp.zeros((row_width, slot_count), jnp.float32)
        .at[:, position]
        .set(rotor_side)
        .reshape(1, row_width, slot_count)
    )
    values = lax.all_to_all(
        outgoing_values, ("rotor", "stator"), split_axis=2, concat_axis=2, tiled=True
    )
    arrived_codes = lax.all_to_all(
        outgoing_codes, ("rotor", "stator"), split_axis=2, concat_axis=2, tiled=True
    )
    batch = values.shape[0]
    slots = values.shape[2]
    filled = arrived_codes[:, 0, :] >= 0
    row_index = jnp.where(filled, arrived_codes[:, 0, :] // 2, 0)
    arrived_sides = jnp.where(filled, arrived_codes[:, 0, :] % 2, 0)
    gathered = stator_faces[:, :, row_index]
    both = jnp.einsum("sij,vjbk->svibk", proj_stator, gathered, precision=TOP_PRECISION)
    stator_side = jnp.where((arrived_sides == 0)[None, None], both[0], both[1])
    rotor_values = jnp.moveaxis(values.reshape(batch, 5, surface_nodes, slots), 0, 2)
    safe_rotor = jnp.where(filled[None, None], rotor_values, stator_side)
    flux_values = jnp.where(filled[None, None], rusanov_leading(safe_rotor, stator_side), 0.0)
    adjoint = jnp.einsum("sji,vjbk->svibk", proj_stator, flux_values, precision=TOP_PRECISION)
    stator_part = 0.5 * jnp.where((arrived_sides == 0)[None, None], adjoint[0], adjoint[1])
    flux_rows = jnp.moveaxis(flux_values, 2, 0).reshape(batch, row_width, slots)
    returned = lax.all_to_all(
        flux_rows, ("rotor", "stator"), split_axis=2, concat_axis=2, tiled=True
    )
    returned, stator_part, row_index = (
        returned,
        jnp.moveaxis(stator_part, 2, 0).reshape(batch, row_width, slots),
        row_index,
    )
    segment_flux = returned.reshape(row_width, slot_count)[:, position].reshape(
        5, surface_nodes, 2, elements
    )
    stator_flux = (
        jnp.zeros((row_width, elements), jnp.float32)
        .at[:, row_index.reshape(slot_count)]
        .add(stator_part.reshape(row_width, slot_count))
    )
    stator_flux = stator_flux.reshape(5, NODES, NODES, elements)
    owner_placed = lax.all_to_all(
        segment_flux.reshape(5, surface_nodes, 2, rotors, band_rows),
        "rotor",
        split_axis=3,
        concat_axis=3,
        tiled=True,
    ).reshape(5, surface_nodes, 2, elements)
    rotor_face_flux = 0.5 * jnp.einsum(
        "sjo,vjsf->vof", rotor_projection, owner_placed, precision=TOP_PRECISION
    )
    rotor_face_flux = rotor_face_flux.reshape(5, NODES, NODES, elements)
    rotor_rate = volume_rate(rotor_state, matrix)
    stator_rate = volume_rate(stator_state, matrix)
    rotor_rate = rotor_rate.at[:, :, :, NODES - 1, :].add(
        -LIFT_FACTOR * (rotor_face_flux - face_flux(rotor_state[:, :, :, NODES - 1, :]))
    )
    stator_rate = stator_rate.at[:, :, :, 0, :].add(
        LIFT_FACTOR * (stator_flux - face_flux(stator_state[:, :, :, 0, :]))
    )
    return (rotor_state + TIME_STEP * rotor_rate, stator_state + TIME_STEP * stator_rate)


def solution(mesh):
    in_specs = (
        P(None, None, None, None, ("rotor", "stator")),
        P(None, None, None, None, ("rotor", "stator")),
        P(),
        P(),
        P(("rotor", "stator"), None),
        P(("rotor", "stator")),
    )
    out_specs = (
        P(None, None, None, None, ("rotor", "stator")),
        P(None, None, None, None, ("rotor", "stator")),
    )
    return jax.shard_map(body, mesh=mesh, in_specs=in_specs, out_specs=out_specs, check_vma=False)
```

profile of v0, /device:TPU:1, one launch (start us, length us, event | category | flops | bytes accessed | tf_op | source)
XLA Modules:
  0.0 335.1 jit_solution(17783389726861730281)
XLA Ops:
  0.6 2.6 slice.208
  3.2 2.7 convolution_bitcast_fusion.1
  6.0 2.1 reshape.1120
  8.1 2.0 copy.290
  10.0 3.3 reshape.1193
  13.3 6.5 %all-to-all-start.1 = ((f32[8,1,30720]{2,1,0:T(1,128)}), f32[8,1,30720]{2,1,0:T(1,128)}, u32[]{:S(2)}, u32[]{:S(2)}) async-start(f32[8,1,30720]{2,1,0:T(1,128)} %reshape.1193), calls=%async_computation.1 | async-start | bytes 1966080 | tf_op jit(solution)/shard_map/all_to_all | solution.py:100
  20.3 4.5 %copy.344 = f32[5,8,8,8,384]{4,1,3,2,0:T(8,128)S(1)} copy(f32[5,8,8,8,384]{4,3,2,1,0:T(8,128)} %param.12) | data formatting | bytes 7864320 | tf_op args[1]
  26.9 2.2 copy.324
  33.6 3.6 %add_dynamic-update-slice_fusion.2 = (f32[5,8,8,8,384]{4,1,3,2,0:T(8,128)}, f32[1,8,8,8,384]{4,1,3,2,0:T(8,128)S(1)}, f32[1,8,8,8,384]{4,1,3,2,0:T(8,128)S(1)}, ...) fusion(f32[5,8,8,8,384]{4,1,3,2,0:T(8,128)} %slice_dynamic-update-slice_fusion.2, f32[5,8,8,8,384]{4,1,3,2,0:T(8,128)} %copy-done.3), kind=kLoop, calls=%fused_computation.60 | loop fusion | flops 2555904 | bytes 7864320
  39.8 1.3 multiply_dynamic-update-slice_fusion.6
  43.1 3.5 %copy-done.9 = f32[5,8,8,8,384]{4,1,3,2,0:T(8,128)S(1)} copy-done((f32[5,8,8,8,384]{4,1,3,2,0:T(8,128)S(1)}, f32[5,8,8,8,384]{4,1,3,2,0:T(8,128)}, u32[]{:S(2)}) %copy-start.9) | copy-done | bytes 3932184
  54.5 3.4 %scatter_custom_fusion = s32[1536]{0:T(1024)S(1)} fusion(s32[768]{0:T(1024)S(1)} %fusion.77, s32[768]{0:T(1024)S(1)} %fusion.71, s32[]{:T(128)} %constant.121.clone.1), kind=kCustom, calls=%fused_computation.220 | custom fusion | bytes 6148 | tf_op jit(solution)/shard_map/scatter | solution.py:118
  57.8 5.4 %reshape.1178 = s32[1,1,1536]{1,0,2:T(1,128)} reshape(s32[1536]{0:T(1024)S(1)} %scatter_custom_fusion) | data formatting | bytes 12288 | tf_op jit(solution)/shard_map/reshape | solution.py:119
  63.2 1.8 constant_dynamic-update-slice_fusion.5
  65.1 2.2 multiply_dynamic-update-slice_fusion.3
  67.2 2.1 multiply_dynamic-update-slice_fusion.12
  69.4 11.1 %all-to-all-start = ((s32[1,1,1536]{1,0,2:T(1,128)}), s32[1,1,1536]{1,0,2:T(1,128)}, u32[]{:S(2)}, u32[]{:S(2)}) async-start(s32[1,1,1536]{1,0,2:T(1,128)} %reshape.1178), calls=%async_computation | async-start | bytes 1572864 | tf_op jit(solution)/shard_map/all_to_all | solution.py:130
  80.5 1.5 constant_dynamic-update-slice_fusion.9
  82.6 4.2 %reduce.14 = f32[8,30720]{1,0:T(8,128)S(1)} reduce(f32[8,1,30720]{2,1,0:T(1,128)} %all-to-all-done.1, f32[]{:T(128)} %broadcast.803), dimensions={1}, to_apply=%all_to_all.16.reduce_sub_computation | reduce | bytes 1966084 | tf_op jit(solution)/shard_map/all_to_all | solution.py:100
  86.8 2.1 reshape.1194
  88.9 2.2 copy.291
  91.1 2.2 reshape.1153
  93.2 2.6 copy.292
  95.8 6.6 %scatter_custom_fusion.1 = f32[320,1536]{0,1:T(8,128)S(1)} fusion(s32[768]{0:T(1024)S(1)} %fusion.77, f32[768,320]{1,0:T(8,128)} %copy.292, f32[]{:T(128)} %constant.128.clone.1), kind=kCustom, calls=%fused_computation.41 | custom fusion | bytes 1966592 | tf_op jit(solution)/shard_map/scatter | solution.py:124
  102.4 8.2 %copy.293 = f32[1,320,1536]{1,0,2:T(1,128)} copy(f32[1,320,1536]{1,2,0:T(8,128)S(1)} %bitcast.196) | data formatting | bytes 3932160 | tf_op jit(solution)/shard_map/reshape | solution.py:125
  110.6 10.2 %all-to-all-start.2 = ((f32[1,320,1536]{1,0,2:T(1,128)}), f32[1,320,1536]{1,0,2:T(1,128)S(1)}, u32[]{:S(2)}, u32[]{:S(2)}) async-start(f32[1,320,1536]{1,0,2:T(1,128)} %copy.293), calls=%async_computation.2 | async-start | bytes 4718592 | tf_op jit(solution)/shard_map/all_to_all | solution.py:127
  120.7 1.5 constant_dynamic-update-slice_fusion.4
  122.3 1.7 copy.296
  124.1 9.7 %fusion.6 = f32[5,8,8,384,8]{3,4,2,1,0:T(8,128)} fusion(f32[8,8,1,1,1]{1,0,4,3,2:T(8,128)S(1)} %copy-done.23, f32[5,8,8,8,384]{4,1,3,2,0:T(8,128)} %multiply_dynamic-update-slice_fusion.3), kind=kOutput, calls=%fused_computation.16 | convolution fusion | flops 94371840 | bytes 7864576 | tf_op jit(solution)/shard_map/ij,vajce->vaice/dot_general | solution.py:75
  133.8 5.7 %fusion.4 = f32[5,8,8,384,8]{3,4,2,1,0:T(8,128)} fusion(f32[8,8,1,1,1]{1,0,4,3,2:T(8,128)S(1)} %copy-done.23, f32[5,8,8,8,384]{4,1,3,2,0:T(8,128)S(1)} %copy-done.14), kind=kOutput, calls=%fused_computation.14 | convolution fusion | flops 94371840 | bytes 7864576 | tf_op jit(solution)/shard_map/ij,vabje->vabie/dot_general | solution.py:75
  139.5 9.8 %fusion.10 = f32[5,8,8,384,8]{3,4,2,1,0:T(8,128)} fusion(f32[8,8,1,1,1]{1,0,4,3,2:T(8,128)S(1)} %copy-done.23, f32[5,8,8,8,384]{4,1,3,2,0:T(8,128)} %multiply_dynamic-update-slice_fusion.12), kind=kOutput, calls=%fused_computation.20 | convolution fusion | flops 94371840 | bytes 7864576 | tf_op jit(solution)/shard_map/ij,vajce->vaice/dot_general | solution.py:75
  149.2 29.8 %reduce.6 = s32[1536]{0:T(1024)S(1)} reduce(s32[1,1,1536]{1,0,2:T(1,128)} %all-to-all-done, s32[]{:T(128)} %constant.123.clone.1), dimensions={0,1}, to_apply=%all_to_all.15.reduce_sub_computation | reduce | bytes 12292 | tf_op jit(solution)/shard_map/all_to_all | solution.py:130
  179.2 5.9 %gather_fusion = f32[1536,5,64]{2,1,0:T(8,128)} fusion(f32[5,64,384]{1,0,2:T(8,128)} %copy.296, s32[2048]{0:T(1024)S(1)} %pad_clamp_fusion), kind=kCustom, calls=%fused_computation | custom fusion | bytes 3938304 | tf_op jit(solution)/shard_map/gather | solution.py:138
  185.1 8.9 %fusion.12 = f32[2,5,64,1,1536]{4,2,0,1,3:T(8,128)} fusion(f32[5,64,1536,1]{1,0,2,3:T(8,128)} %bitcast.204, f32[2,64,64]{2,1,0:T(8,128)S(1)} %copy-done), kind=kOutput, calls=%fused_computation.24 | convolution fusion | flops 754974720 | bytes 5931008 | tf_op jit(solution)/shard_map/sij,vjbk->svibk/dot_general | solution.py:139
  194.0 5.1 %copy.294 = f32[1,320,1536]{2,1,0:T(8,128)} copy(f32[1,320,1536]{1,0,2:T(1,128)S(1)} %all-to-all-done.2) | data formatting | bytes 3932160 | tf_op jit(solution)/shard_map/all_to_all | solution.py:127
  199.0 3.3 broadcast_select_fusion.1
  206.4 6.0 %copy.311 = f32[1,320,1536]{1,0,2:T(1,128)S(1)} copy(f32[1,320,1536]{2,1,0:T(8,128)} %bitcast.207) | data formatting | bytes 3932160 | tf_op jit(solution)/shard_map/stack | solution.py:65
  212.4 6.4 %broadcast_select_fusion = f32[1,320,1536]{1,0,2:T(1,128)} fusion(f32[1,320,1536]{1,0,2:T(1,128)S(1)} %copy.311, pred[1536]{0:T(1024)(128)(4,1)S(1)} %get-tuple-element.94), kind=kLoop, calls=%fused_computation.5 | loop fusion | flops 491520 | bytes 3933696 | tf_op jit(solution)/shard_map/jit(_where)/select_n | solution.py:143
  218.8 10.3 %all-to-all-start.3 = ((f32[1,320,1536]{1,0,2:T(1,128)}), f32[1,320,1536]{1,0,2:T(1,128)}, u32[]{:S(2)}, u32[]{:S(2)}) async-start(f32[1,320,1536]{1,0,2:T(1,128)} %broadcast_select_fusion), calls=%async_computation.3 | async-start | bytes 4718592 | tf_op jit(solution)/shard_map/all_to_all | solution.py:147
  229.2 6.2 %fusion.8 = f32[5,8,8,384,8]{3,4,2,1,0:T(8,128)S(1)} fusion(f32[8,8,1,1,1]{1,0,4,3,2:T(8,128)S(1)} %copy-done.23, f32[5,8,8,8,384]{4,1,3,2,0:T(8,128)} %copy-done.15), kind=kOutput, calls=%fused_computation.18 | convolution fusion | flops 94371840 | bytes 7864576 | tf_op jit(solution)/shard_map/ij,vabje->vabie/dot_general | solution.py:75
  235.5 12.0 %fusion = f32[5,8,8,8,384]{4,1,3,2,0:T(8,128)} fusion(f32[5,8,8,384,8]{3,4,2,1,0:T(8,128)S(1)} %copy-done.8, f32[5,8,8,384,8]{3,4,2,1,0:T(8,128)S(1)} %copy-done.7, f32[5,8,8,8,384]{4,1,3,2,0:T(8,128)} %get-tuple-element.71, f32[8,8,1,1,1]{1,0,4,3,2:T(8,128)S(1)} %copy-done.23), kind=kOutput, calls=%fused_computation.7 | convolution fusion | flops 97320960 | bytes 15728896 | tf_op jit(solution)/shard_map/ij,vjbce->vibce/dot_general | solution.py:75
  247.5 10.2 %fusion.3 = f32[5,8,8,8,384]{4,1,3,2,0:T(8,128)} fusion(f32[5,8,8,384,8]{3,4,2,1,0:T(8,128)S(1)} %fusion.8, f32[5,8,8,384,8]{3,4,2,1,0:T(8,128)S(1)} %copy-done.6, f32[5,8,8,8,384]{4,1,3,2,0:T(8,128)S(1)} %copy-done.11, f32[8,8,1,1,1]{1,0,4,3,2:T(8,128)S(1)} %copy-done.23), kind=kOutput, calls=%fused_computation.12 | convolution fusion | flops 97320960 | bytes 15728896 | tf_op jit(solution)/shard_map/ij,vjbce->vibce/dot_general | solution.py:75
  257.8 5.5 %convolution_bitcast_fusion = f32[2,5,64,1,1536]{4,2,0,1,3:T(8,128)} fusion(f32[5,64,1536]{2,1,0:T(8,128)S(1)} %copy-done.18, pred[1536]{0:T(1024)(128)(4,1)S(1)} %get-tuple-element.94, f32[2,64,64]{2,1,0:T(8,128)S(1)} %copy-done), kind=kOutput, calls=%fused_computation.25 | convolution fusion | flops 755466240 | bytes 5932544 | tf_op jit(solution)/shard_map/sji,vjbk->svibk/dot_general | solution.py:144
  263.3 1.8 copy.398
  265.1 3.0 gather_fusion.1
  268.2 2.3 reshape.1179
  270.4 1.6 copy.400
  272.1 3.4 %reshape.1195 = f32[8,1,30720]{2,1,0:T(1,128)} reshape(f32[8,5,2,48,64]{4,3,2,1,0:T(8,128)} %bitcast.200) | data formatting | bytes 1966080
  275.4 4.8 %all-to-all-start.4 = ((f32[8,1,30720]{2,1,0:T(1,128)}), f32[8,1,30720]{2,1,0:T(1,128)S(1)}, u32[]{:S(2)}, u32[]{:S(2)}) async-start(f32[8,1,30720]{2,1,0:T(1,128)} %reshape.1195), calls=%async_computation.4 | async-start | bytes 1966080 | tf_op jit(solution)/shard_map/all_to_all | solution.py:164
  280.3 4.3 %fusion.85 = (f32[1,5,64,1,1536]{4,2,0,1,3:T(8,128)}, f32[1,5,64,1,1536]{4,2,0,1,3:T(8,128)}) fusion(f32[2,5,64,1,1536]{4,2,0,1,3:T(8,128)} %convolution_bitcast_fusion), kind=kLoop, calls=%fused_computation.227 | loop fusion | bytes 7864320 | tf_op jit(solution)/shard_map/slice | solution.py:145
  284.5 2.0 copy.335
  286.5 3.0 copy.336
  289.5 11.9 %scatter_custom_fusion.2 = f32[320,384]{0,1:T(8,128)} fusion(s32[1536]{0:T(1024)S(1)} %fusion.70, f32[320,1536]{0,1:T(8,128)S(1)} %copy.335, f32[320,1536]{0,1:T(8,128)} %copy.336, f32[]{:T(128)} %constant.119.clone.1, pred[1536]{0:T(1024)(128)(4,1)S(1)} %get-tuple-element.93, f32[]{:T(128)} %constant.128.clone.1), kind=kCustom, calls=%fused_computation.26 | custom fusion | flops 1474560 | bytes 4818952 | tf_op jit(solution)/shard_map/scatter-add | solution.py:161
  302.7 2.1 fusion.32
  304.8 5.8 %multiply_add_fusion = f32[5,8,8,8,384]{4,1,3,2,0:T(8,128)S(1)} fusion(f32[5,8,8,8,384]{4,1,3,2,0:T(8,128)} %fusion.32, f32[5,8,8,8,384]{4,3,2,1,0:T(8,128)} %param.12), kind=kLoop, calls=%fused_computation.22 | loop fusion | flops 1966080 | bytes 11796480 | tf_op jit(solution)/shard_map/add | solution.py:183
  310.6 2.6 copy.346
  313.3 3.0 reduce.15
  316.3 2.1 reshape.1196
  318.4 2.4 copy.316
  320.7 1.7 reshape.1125
  322.4 1.9 fusion.23
  324.4 2.1 fusion.33
  326.5 5.8 %multiply_add_fusion.1 = f32[5,8,8,8,384]{4,1,3,2,0:T(8,128)S(1)} fusion(f32[5,8,8,8,384]{4,1,3,2,0:T(8,128)} %fusion.33, f32[5,8,8,8,384]{4,3,2,1,0:T(8,128)} %param.11), kind=kLoop, calls=%fused_computation.23 | loop fusion | flops 1966080 | bytes 11796480 | tf_op jit(solution)/shard_map/add | solution.py:183
  332.3 2.6 copy.345
  (117 shorter events, 25.2 us)
Async XLA Ops:
  0.6 184.5 %copy-start = (f32[2,64,64]{2,1,0:T(8,128)S(1)}, f32[2,64,64]{2,1,0:T(8,128)}, u32[]{:S(2)}) copy-start(f32[2,64,64]{2,1,0:T(8,128)} %param.14) | copy-start | bytes 98308
  8.1 11.8 %copy-start.25 = (s32[768,1]{0,1:T(1,128)S(1)}, s32[768,1]{0,1:T(1,128)}, u32[]{:S(2)}) copy-start(s32[768,1]{0,1:T(1,128)} %param.15) | copy-start | bytes 9220
  13.3 56.0 %all-to-all-start.1 = ((f32[8,1,30720]{2,1,0:T(1,128)}), f32[8,1,30720]{2,1,0:T(1,128)}, u32[]{:S(2)}, u32[]{:S(2)}) async-start(f32[8,1,30720]{2,1,0:T(1,128)} %reshape.1193), calls=%async_computation.1 | async-start | bytes 1966080 | tf_op jit(solution)/shard_map/all_to_all | solution.py:100
  20.2 6.6 %copy-start.5 = (f32[5,8,8,8,384]{4,3,2,1,0:T(8,128)S(1)}, f32[5,8,8,8,384]{4,3,2,1,0:T(8,128)}, u32[]{:S(2)}) copy-start(f32[5,8,8,8,384]{4,3,2,1,0:T(8,128)} %param.11) | copy-start | bytes 11796484
  24.8 2.1 copy-start.3
  29.1 2.0 copy-start.1
  29.1 4.1 %copy-start.24 = (s32[768]{0:T(1024)S(1)}, s32[768]{0:T(1024)}, u32[]{:S(2)}) copy-start(s32[768]{0:T(1024)} %param.16) | copy-start | bytes 9220
  33.6 3.6 %copy-start.4 = (f32[5,8,8,8,384]{4,1,3,2,0:T(8,128)S(1)}, f32[5,8,8,8,384]{4,1,3,2,0:T(8,128)}, u32[]{:S(2)}) copy-start(f32[5,8,8,8,384]{4,1,3,2,0:T(8,128)} %copy-done.3) | copy-start | bytes 11796484
  39.8 2.7 copy-start.2
  41.1 6.0 %copy-start.13 = (f32[5,8,8,8,384]{4,1,3,2,0:T(8,128)}, f32[5,8,8,8,384]{4,1,3,2,0:T(8,128)S(1)}, u32[]{:S(2)}) copy-start(f32[5,8,8,8,384]{4,1,3,2,0:T(8,128)S(1)} %get-tuple-element.72) | copy-start | bytes 11796484
  41.1 5.5 %copy-start.9 = (f32[5,8,8,8,384]{4,1,3,2,0:T(8,128)S(1)}, f32[5,8,8,8,384]{4,1,3,2,0:T(8,128)}, u32[]{:S(2)}) copy-start(f32[5,8,8,8,384]{4,1,3,2,0:T(8,128)} %slice_dynamic-update-slice_fusion.5) | copy-start | bytes 11796484
  41.3 5.9 %copy-start.12 = (f32[5,8,8,8,384]{4,1,3,2,0:T(8,128)}, f32[5,8,8,8,384]{4,1,3,2,0:T(8,128)S(1)}, u32[]{:S(2)}) copy-start(f32[5,8,8,8,384]{4,1,3,2,0:T(8,128)S(1)} %multiply_dynamic-update-slice_fusion.4) | copy-start | bytes 11796484
  41.4 0.8 copy-start.20
  49.7 2.4 copy-start.19
  51.0 2.7 copy-start.10
  51.0 3.5 %copy-start.15 = (f32[5,8,8,8,384]{4,1,3,2,0:T(8,128)}, f32[5,8,8,8,384]{4,1,3,2,0:T(8,128)S(1)}, u32[]{:S(2)}) copy-start(f32[5,8,8,8,384]{4,1,3,2,0:T(8,128)S(1)} %get-tuple-element.75) | copy-start | bytes 11796484
  69.4 41.2 %all-to-all-start = ((s32[1,1,1536]{1,0,2:T(1,128)}), s32[1,1,1536]{1,0,2:T(1,128)}, u32[]{:S(2)}, u32[]{:S(2)}) async-start(s32[1,1,1536]{1,0,2:T(1,128)} %reshape.1178), calls=%async_computation | async-start | bytes 1572864 | tf_op jit(solution)/shard_map/all_to_all | solution.py:130
  102.4 18.4 %copy-start.21 = (f32[1,8,8,1,384]{4,1,3,2,0:T(8,128)S(1)}, f32[1,8,8,1,384]{4,1,3,2,0:T(8,128)}, u32[]{:S(2)}) copy-start(f32[1,8,8,1,384]{4,1,3,2,0:T(8,128)} %get-tuple-element.63) | copy-start | bytes 294916
  110.6 11.7 %slice-start = ((f32[5,8,8,8,384]{4,3,2,1,0:T(8,128)}), f32[5,8,8,1,384]{4,3,2,1,0:T(1,128)S(1)}, s32[]{:S(2)}) async-start(f32[5,8,8,8,384]{4,3,2,1,0:T(8,128)} %param.12), calls=%async_computation.5 | async-start | bytes 983040 | tf_op jit(solution)/shard_map/slice | solution.py:108
  110.6 13.5 %copy-start.23 = (f32[8,8,1,1,1]{1,0,4,3,2:T(8,128)S(1)}, f32[8,8,1,1,1]{1,0,4,3,2:T(8,128)}, u32[]{:S(2)}) copy-start(f32[8,8,1,1,1]{1,0,4,3,2:T(8,128)} %constant.135) | copy-start | bytes 772
  110.6 83.4 %all-to-all-start.2 = ((f32[1,320,1536]{1,0,2:T(1,128)}), f32[1,320,1536]{1,0,2:T(1,128)S(1)}, u32[]{:S(2)}, u32[]{:S(2)}) async-start(f32[1,320,1536]{1,0,2:T(1,128)} %copy.293), calls=%async_computation.2 | async-start | bytes 4718592 | tf_op jit(solution)/shard_map/all_to_all | solution.py:127
  124.1 9.7 %copy-start.14 = (f32[5,8,8,8,384]{4,1,3,2,0:T(8,128)S(1)}, f32[5,8,8,8,384]{4,1,3,2,0:T(8,128)}, u32[]{:S(2)}) copy-start(f32[5,8,8,8,384]{4,1,3,2,0:T(8,128)} %copy-done.13) | copy-start | bytes 11796484
  203.8 1.3 copy-start.17
  205.1 1.3 copy-start.16
  218.8 44.5 %all-to-all-start.3 = ((f32[1,320,1536]{1,0,2:T(1,128)}), f32[1,320,1536]{1,0,2:T(1,128)}, u32[]{:S(2)}, u32[]{:S(2)}) async-start(f32[1,320,1536]{1,0,2:T(1,128)} %broadcast_select_fusion), calls=%async_computation.3 | async-start | bytes 4718592 | tf_op jit(solution)/shard_map/all_to_all | solution.py:147
  229.2 6.3 %copy-start.7 = (f32[5,8,8,384,8]{3,4,2,1,0:T(8,128)S(1)}, f32[5,8,8,384,8]{3,4,2,1,0:T(8,128)}, u32[]{:S(2)}) copy-start(f32[5,8,8,384,8]{3,4,2,1,0:T(8,128)} %fusion.6) | copy-start | bytes 11796484
  229.2 6.3 %copy-start.8 = (f32[5,8,8,384,8]{3,4,2,1,0:T(8,128)S(1)}, f32[5,8,8,384,8]{3,4,2,1,0:T(8,128)}, u32[]{:S(2)}) copy-start(f32[5,8,8,384,8]{3,4,2,1,0:T(8,128)} %fusion.4) | copy-start | bytes 11796484
  235.4 12.1 %copy-start.6 = (f32[5,8,8,384,8]{3,4,2,1,0:T(8,128)S(1)}, f32[5,8,8,384,8]{3,4,2,1,0:T(8,128)}, u32[]{:S(2)}) copy-start(f32[5,8,8,384,8]{3,4,2,1,0:T(8,128)} %fusion.10) | copy-start | bytes 11796484
  235.5 12.1 %copy-start.11 = (f32[5,8,8,8,384]{4,1,3,2,0:T(8,128)S(1)}, f32[5,8,8,8,384]{4,1,3,2,0:T(8,128)}, u32[]{:S(2)}) copy-start(f32[5,8,8,8,384]{4,1,3,2,0:T(8,128)} %copy-done.10) | copy-start | bytes 11796484
  247.5 10.3 %copy-start.18 = (f32[5,64,1536]{2,1,0:T(8,128)S(1)}, f32[5,64,1536]{2,1,0:T(8,128)}, u32[]{:S(2)}) copy-start(f32[5,64,1536]{2,1,0:T(8,128)} %copy-done.17) | copy-start | bytes 5898244
  275.4 37.8 %all-to-all-start.4 = ((f32[8,1,30720]{2,1,0:T(1,128)}), f32[8,1,30720]{2,1,0:T(1,128)S(1)}, u32[]{:S(2)}, u32[]{:S(2)}) async-start(f32[8,1,30720]{2,1,0:T(1,128)} %reshape.1195), calls=%async_computation.4 | async-start | bytes 1966080 | tf_op jit(solution)/shard_map/all_to_all | solution.py:164
  318.4 4.1 %copy-start.22 = (f32[2,64,64]{2,1,0:T(8,128)S(1)}, f32[2,64,64]{2,1,0:T(8,128)}, u32[]{:S(2)}) copy-start(f32[2,64,64]{2,1,0:T(8,128)} %param.13) | copy-start | bytes 98308
where the time goes:
time: 340 us; the launch traced here: 335 us
  local copies, waits for them, and re-layouts  117 us (34%)
  other arithmetic  101 us (30%)
  matrix products  72.6 us (21%)
  starting transfers between devices  42.9 us (13%)
    dot_general x6, matrix products, volume_rate(): jnp.einsum(patterns[direction], matrix, flux_values, precision=TOP_PRECIS...  53.7 us
    unnamed x70, local copies, waits for them, and re-layouts  35.8 us
    all_to_all x1, other arithmetic, body(): lax.all_to_all(outgoing_codes, ('rotor', 'stator'), split_axis=2, concat_...  29.8 us
    unnamed x24, other arithmetic  15.5 us
    scatter-add x1, other arithmetic, body(): stator_flux = jnp.zeros((row_width, elements), jnp.float32).at[:, row_ind...  11.9 us
    all_to_all x1, starting transfers between devices, body(): lax.all_to_all(outgoing_codes, ('rotor', 'stator'), split_axis=2, concat_...  11.1 us
    all_to_all x1, starting transfers between devices, body(): lax.all_to_all(flux_rows, ('rotor', 'stator'), split_axis=2, concat_axis=...  10.3 us
    all_to_all x1, starting transfers between devices, body(): lax.all_to_all(outgoing_values, ('rotor', 'stator'), split_axis=2, concat...  10.2 us
  transfers between devices with their start and end apart: 5, of which 0 were waited for; matrix products, arithmetic and copies ran while one was open for 63% of the time, Pallas kernels for 0%

commit v1 on v0

v1 whole, which is shorter than its diff:
```python
import functools

import jax
import jax.numpy as jnp
import numpy as np
from jax import lax
from jax.experimental import pallas as pl
from jax.experimental.pallas import tpu as pltpu
from jax.sharding import PartitionSpec as P

NODES = 8
FACE = 64
NR = 8
NS = 16
ND = NR * NS
ELEMS = 384
BAND = ELEMS // NR
SEGS = 2 * ELEMS
ROWS = 5 * NODES * FACE
CAP = 12
PAIRS = CAP // 2
HALF = PAIRS // 2
MSG = 16
CHUNK_ROWS = ND * MSG
WIDE = 5 * 128
GAMMA = 1.4
TIME_STEP = 0.02
LIFT = 28.0
MESH = pl.DeviceIdType.MESH
F32 = jnp.float32
BF16 = jnp.bfloat16


def cheb_matrix():
    degree = NODES - 1
    j = np.arange(degree + 1)
    points = -np.cos(np.pi * j / degree)
    weights = np.where((j == 0) | (j == degree), 2.0, 1.0) * (-1.0) ** j
    spacing = points[:, None] - points[None, :]
    identity = np.eye(degree + 1)
    matrix = weights[:, None] / weights[None, :] / (spacing + identity)
    matrix = matrix - identity * matrix.sum(axis=1)[:, None]
    return matrix.astype(np.float32)


DM = cheb_matrix().astype(np.float64) * (-TIME_STEP * 0.5)
ODD = DM[:4, :4] - DM[:4, :3:-1]
EVEN = DM[:4, :4] + DM[:4, :3:-1]


def derive(line):
    plus = [line[j] + line[7 - j] for j in range(4)]
    minus = [line[j] - line[7 - j] for j in range(4)]
    out = [None] * 8
    for i in range(4):
        p = sum(float(ODD[i, j]) * minus[j] for j in range(4))
        q = sum(float(EVEN[i, j]) * plus[j] for j in range(4))
        out[i] = p + q
        out[7 - i] = p - q
    return out


def primitive(fields):
    density, mx, my, mz, energy = fields
    inverse = 1.0 / density
    u = (mx * inverse, my * inverse, mz * inverse)
    kinetic = mx * u[0] + my * u[1] + mz * u[2]
    return u, (GAMMA - 1.0) * (energy - 0.5 * kinetic), inverse


def flux_along(fields, speed, pressure, direction):
    result = [fields[1 + direction]]
    for k in range(3):
        term = fields[1 + k] * speed
        result.append(term + pressure if k == direction else term)
    result.append((fields[4] + pressure) * speed)
    return result


def rusanov(left, right):
    lu, lp, li = primitive(left)
    ru, rp, ri = primitive(right)
    lf = flux_along(left, lu[2], lp, 2)
    rf = flux_along(right, ru[2], rp, 2)
    signal = jnp.maximum(
        jnp.abs(lu[2]) + jnp.sqrt(GAMMA * lp * li), jnp.abs(ru[2]) + jnp.sqrt(GAMMA * rp * ri)
    )
    return [
        0.5 * (lf[v] + rf[v]) - 0.5 * signal * (right[v] - left[v]) for v in range(5)
    ]


def split(x):
    hi = x.astype(BF16)
    return hi, (x - hi.astype(F32)).astype(BF16)


def dot_nn(a, b):
    return lax.dot_general(a, b, (((1,), (0,)), ((), ())), preferred_element_type=F32)


def dot_nt(a, b):
    return lax.dot_general(a, b, (((1,), (1,)), ((), ())), preferred_element_type=F32)


def dot3(dot, a, b):
    return dot(a[0], b[0]) + dot(a[0], b[1]) + dot(a[1], b[0])


def hot(mask):
    return jnp.where(mask, 1.0, 0.0).astype(BF16)


def iota(shape, dim):
    return lax.broadcasted_iota(jnp.int32, shape, dim)


def volume_first(src, prim, tmp, acc, step):
    t, a = lax.div(step, 8), lax.rem(step, 8)
    at = lambda v, b: pl.ds(pl.multiple_of(v * 512 + a * 64 + b * 8, 8), 8)
    lines = [[] for _ in range(5)]
    for b in range(8):
        fields = [src[t, at(v, b), :] for v in range(5)]
        u, p, _ = primitive(fields)
        prim[at(0, b), :] = u[0]
        prim[at(1, b), :] = u[2]
        prim[at(2, b), :] = p
        for v, value in enumerate(flux_along(fields, u[1], p, 1)):
            lines[v].append(value)
    for v in range(5):
        for b, value in enumerate(derive(lines[v])):
            acc[at(v, b), :] = value
    column = lambda v, c: pl.ds(v * 512 + a * 64 + c, 8, stride=8)
    lines = [[] for _ in range(5)]
    for c in range(8):
        fields = [None] + [src[t, column(v, c), :] for v in range(1, 5)]
        for v, value in enumerate(
            flux_along(fields, prim[column(1, c), :], prim[column(2, c), :], 2)
        ):
            lines[v].append(value)
    for v in range(5):
        for c, value in enumerate(derive(lines[v])):
            tmp[pl.ds(v * 64 + c, 8, stride=8), :] = value
    for v in range(5):
        for b in range(8):
            acc[at(v, b), :] += tmp[v * 64 + b * 8 : v * 64 + b * 8 + 8, :]


def volume_second(src, prim, acc, out, t, b):
    at = lambda v, a: pl.ds(pl.multiple_of(v * 512 + a * 64 + b * 8, 8), 8)
    lines = [[] for _ in range(5)]
    for a in range(8):
        fields = [None] + [src[t, at(v, a), :] for v in range(1, 5)]
        for v, value in enumerate(
            flux_along(fields, prim[at(0, a), :], prim[at(2, a), :], 0)
        ):
            lines[v].append(value)
    for v in range(5):
        for a, value in enumerate(derive(lines[v])):
            out[t, at(v, a), :] = src[t, at(v, a), :] + (acc[at(v, a), :] + value)


def volume(src, out, prim, tmp, acc, tiles):
    for t in tiles:

        def first(a, carry):
            volume_first(src, prim, tmp, acc, t * 8 + a)
            return carry

        def second(b, carry):
            volume_second(src, prim, acc, out, t, b)
            return carry

        lax.fori_loop(0, 8, first, 0)
        lax.fori_loop(0, 8, second, 0)


def face_rows(src, node, dst):
    for t in range(3):
        count = 128 if t < 2 else 64
        rows = [
            src[g, pl.ds(t * 1024 + node, count, stride=8), :]
            for g in range(3)
        ]
        for g in range(3):
            block = rows[g]
            if t == 2:
                block = jnp.concatenate([block, jnp.zeros((64, 128), F32)], axis=0)
            dst[g * 128 : g * 128 + 128, t * 128 : t * 128 + 128] = block.T


def place(matrix, half):
    zero = jnp.zeros((FACE, FACE), F32)
    return jnp.concatenate([matrix, zero] if half == 0 else [zero, matrix], axis=1)


def make_table(faces, proj, hi_ref, lo_ref, side_ref):
    zero = jnp.zeros((FACE, 128), F32)
    lower = iota((128, 128), 1) < FACE
    for s in range(2):
        kept = []
        for vh in range(2):
            block = place(proj[s], vh)
            for par in range(2):
                kept.append(jnp.concatenate([block, zero] if par == 0 else [zero, block], axis=0))
        weights = split(jnp.concatenate(kept, axis=0))
        for t in range(3):
            count = 512 if t < 2 else 256
            w = (weights[0][:count], weights[1][:count])

            def body(g, carry):
                rows = pl.ds(pl.multiple_of(g * 128, 128), 128)
                x = split(faces[rows, t * 128 : t * 128 + 128])
                y = dot3(dot_nt, x, w)
                for vh in range(count // 256):
                    v = 2 * t + vh
                    for par in range(2):
                        piece = y[:, (vh * 2 + par) * 128 : (vh * 2 + par + 1) * 128]
                        hi, lo = split(piece)
                        dst = pl.ds(pl.multiple_of((par * 2 + s) * ELEMS + g * 128, 128), 128)
                        hi_ref[dst, v * 128 : v * 128 + 128] = hi
                        lo_ref[dst, v * 128 : v * 128 + 128] = lo
                        if side_ref is not None and par == s:
                            if s == 0:
                                side_ref[rows, v * 128 : v * 128 + 128] = piece
                            else:
                                side_ref[rows, v * 128 : v * 128 + 128] += piece
                return carry

            lax.fori_loop(0, 3, body, 0)


def gather_chunk(chunk, hots, hi_ref, lo_ref, message):
    x = hots[...]
    for v in range(5):
        cols = slice(v * 128, v * 128 + 128)
        y = dot_nn(x, hi_ref[:, cols]) + dot_nn(x, lo_ref[:, cols])
        for pp in range(HALF):
            message[pl.ds(chunk * CHUNK_ROWS + v * HALF + pp, ND, stride=MSG), :] = y[
                pp * ND : pp * ND + ND, :
            ]


def mega(
    owner_ref, row_ref, rproj_ref, sproj_ref, rstate, sstate,
    rvol, svol, rsurf, ssurf,
    rs, ss, ru, su, prim, tmp, acc,
    faces_s, faces_r, bands, code_out, code_in, codes, seg,
    tab_hi, tab_lo, ltab_hi, ltab_lo, lside, rside, hots,
    rout, rin, lout, lin, rflux, rflux_in, fluxes_hi, fluxes_lo, sums,
    load_sem, store_sem, own_sem, code_sem, trace_sem, send_sem, r_sem, l_sem, back_sem,
):
    mi, mj = lax.axis_index("rotor"), lax.axis_index("stator")
    me = mi * NS + mj
    tiles = lambda ref, t: ref.at[:, pl.ds(t * 128, 128)]
    loads = [
        [
            pltpu.make_async_copy(tiles(state, t), held.at[t], load_sem.at[n, t])
            for t in range(3)
        ]
        for n, (state, held) in enumerate(((rstate, rs), (sstate, ss)))
    ]
    for copy in loads[0] + loads[1]:
        copy.start()

    def coords(d):
        return (lax.div(d, NS), lax.rem(d, NS))

    def peer(p):
        q = 1 + lax.rem(p + me * 55, ND - 1)
        o = lax.rem(q * 37, ND)
        i = lax.rem(lax.div(o, NS) + mi, NR)
        j = lax.rem(lax.rem(o, NS) + mj, NS)
        return i, j

    barrier = pltpu.get_barrier_semaphore()

    def greet(p, carry):
        pl.semaphore_signal(
            barrier, inc=1, device_id=coords(lax.rem(me + p, ND)), device_id_type=MESH
        )
        return carry

    lax.fori_loop(1, ND, greet, 0)

    owner = owner_ref[...].astype(F32)
    code = row_ref[...]
    lane = iota((1, SEGS), 1)
    side = lax.rem(lane, 2)
    code = code + side * ELEMS + 1
    high = lax.div(code, 4).astype(F32)
    low = lax.rem(code, 4).astype(F32)
    packed = jnp.concatenate([owner, high, low, jnp.zeros((5, SEGS), F32)], axis=0).astype(BF16)
    new = iota((SEGS, SEGS), 0)
    old = iota((SEGS, SEGS), 1)
    order = hot(old == jnp.where(new < ELEMS, 2 * new, 2 * new - 2 * ELEMS + 1))
    by_side = dot_nt(packed, order)
    owner = by_side[0:1]
    member = owner == iota((ND, SEGS), 0).astype(F32)
    member_hot = hot(member)
    earlier = dot_nn(member_hot, hot(new < old))
    rank = jnp.sum(jnp.where(member, earlier, 0.0), axis=0, keepdims=True)
    seg[0:1, :] = owner
    seg[1:2, :] = rank
    seg[2:8, :] = jnp.zeros((6, SEGS), F32)
    ranked = rank == iota((ND, SEGS), 0).astype(F32)
    table = 4.0 * dot_nt(member_hot, jnp.where(ranked, by_side[1:2], 0.0).astype(BF16))
    table = table + dot_nt(member_hot, jnp.where(ranked, by_side[2:3], 0.0).astype(BF16))
    code_out[...] = table.reshape(ND, 1, 128)

    for copy in loads[0]:
        copy.wait()
    face_rows(rs, NODES - 1, faces_r)
    for copy in loads[1]:
        copy.wait()
    face_rows(ss, 0, faces_s)
    make_table(faces_s, sproj_ref, tab_hi, tab_lo, None)
    volume(rs, ru, prim, tmp, acc, range(3))

    pl.semaphore_wait(barrier, ND - 1)

    def send_code(p, carry):
        i, j = peer(p)
        pltpu.make_async_remote_copy(
            src_ref=code_out.at[i * NS + j], dst_ref=code_in.at[me],
            send_sem=code_sem.at[0], recv_sem=code_sem.at[1],
            device_id=(i, j), device_id_type=MESH,
        ).start()
        return carry

    lax.fori_loop(0, ND - 1, send_code, 0)

    def ring(src, dst, sems, me_rows):
        def send(p, carry):
            i = lax.rem(mi + p, NR)
            pltpu.make_async_remote_copy(
                src_ref=src.at[pl.ds(pl.multiple_of(i * BAND, 16), BAND)],
                dst_ref=dst.at[me_rows],
                send_sem=sems.at[0], recv_sem=sems.at[1],
                device_id=(i, mj), device_id_type=MESH,
            ).start()
            return carry

        lax.fori_loop(1, NR, send, 0)

    def ring_wait(dst, sem):
        rows = dst.at[pl.ds(0, (NR - 1) * BAND)]
        pltpu.make_async_copy(rows, rows, sem).wait()

    my_rows = pl.ds(pl.multiple_of(mi * BAND, 16), BAND)
    ring(faces_r, bands, trace_sem, my_rows)
    own = pltpu.make_async_copy(code_out.at[me], code_in.at[me], own_sem.at[0])
    own.start()
    own_trace = pltpu.make_async_copy(faces_r.at[my_rows], bands.at[my_rows], own_sem.at[1])
    own_trace.start()

    volume(ss, su, prim, tmp, acc, range(1))

    own.wait()
    part = code_in.at[pl.ds(0, ND - 1)]
    pltpu.make_async_copy(part, part, code_sem.at[1]).wait()
    codes[...] = code_in[...].reshape(ND, 128)

    def send_chunk(chunk, src, dst, sems):
        def send(p, carry):
            i, j = peer(p)
            at = pl.ds(pl.multiple_of(chunk * CHUNK_ROWS + (i * NS + j) * MSG, MSG), MSG)
            to = pl.ds(pl.multiple_of(chunk * CHUNK_ROWS + me * MSG, MSG), MSG)
            pltpu.make_async_remote_copy(
                src_ref=src.at[at], dst_ref=dst.at[to],
                send_sem=send_sem, recv_sem=sems.at[chunk],
                device_id=(i, j), device_id_type=MESH,
            ).start()
            return carry

        lax.fori_loop(0, ND - 1, send, 0)

    def wait_chunk(chunk, dst, sems):
        rows = dst.at[pl.ds(chunk * CHUNK_ROWS, (ND - 1) * MSG)]
        pltpu.make_async_copy(rows, rows, sems.at[chunk]).wait()

    def own_chunk(chunk, src, dst, sem):
        to = pl.ds(pl.multiple_of(chunk * CHUNK_ROWS + me * MSG, MSG), MSG)
        return pltpu.make_async_copy(src.at[to], dst.at[to], sem)

    for chunk in range(2):
        for pp in range(HALF):
            for par in range(2):
                slot = 2 * (chunk * HALF + pp) + par
                column = codes[:, slot : slot + 1].astype(jnp.int32) - 1
                hots[pp * ND : pp * ND + ND, par * SEGS : par * SEGS + SEGS] = hot(
                    column == iota((ND, SEGS), 1)
                )
        gather_chunk(chunk, hots, tab_hi, tab_lo, rout)
        send_chunk(chunk, rout, rin, r_sem)
        own_chunk(chunk, rout, rin, own_sem.at[2 + chunk]).start()

    own_trace.wait()
    ring_wait(bands, trace_sem.at[1])
    make_table(bands, rproj_ref, ltab_hi, ltab_lo, lside)
    for chunk in range(2):
        belongs = seg[0:1, :] == iota((ND, SEGS), 0).astype(F32)
        for pp in range(HALF):
            for par in range(2):
                slot = 2 * (chunk * HALF + pp) + par
                hots[pp * ND : pp * ND + ND, par * SEGS : par * SEGS + SEGS] = hot(
                    jnp.logical_and(belongs, seg[1:2, :] == float(slot))
                )
        gather_chunk(chunk, hots, ltab_hi, ltab_lo, lout)
        send_chunk(chunk, lout, lin, l_sem)
        own_chunk(chunk, lout, lin, own_sem.at[4 + chunk]).start()

    volume(ss, su, prim, tmp, acc, range(1, 3))
    stores = [
        pltpu.make_async_copy(held.at[t], tiles(vol, t), store_sem.at[n, t])
        for n, (held, vol) in enumerate(((ru, rvol), (su, svol)))
        for t in range(3)
    ]
    for copy in stores:
        copy.start()

    columns = seg[...].T
    for chunk in range(2):
        own_chunk(chunk, rout, rin, own_sem.at[2 + chunk]).wait()
        wait_chunk(chunk, rin, r_sem)
        for pp in range(HALF):
            at = slice((chunk * HALF + pp) * ND, (chunk * HALF + pp + 1) * ND)
            for v in range(5):
                x = rin[pl.ds(chunk * CHUNK_ROWS + v * HALF + pp, ND, stride=MSG), :]
                hi, lo = split(x)
                fluxes_hi[at, v * 128 : v * 128 + 128] = hi
                fluxes_lo[at, v * 128 : v * 128 + 128] = lo
    lower = iota((ELEMS, 128), 1) < FACE
    for s in range(2):
        mine = columns[s * ELEMS : s * ELEMS + ELEMS, :]
        ranks = mine[:, 1:2].astype(jnp.int32)
        owners = mine[:, 0:1].astype(jnp.int32)
        picks = []
        for par in range(2):
            slot = jnp.where(lax.rem(ranks, 2) == par, lax.div(ranks, 2) * ND + owners, -1)
            picks.append(hot(slot == iota((ELEMS, SEGS), 1)))
        for v in range(5):
            cols = slice(v * 128, v * 128 + 128)
            hi, lo = fluxes_hi[:, cols], fluxes_lo[:, cols]
            y = [dot_nn(x, hi) + dot_nn(x, lo) for x in picks]
            y = jnp.where(lower, y[0], y[1])
            y = y + pltpu.roll(y, FACE, 1)
            if s == 0:
                rside[:, cols] = y
            else:
                rside[:, cols] = jnp.where(lower, rside[:, cols], y)
    both = [rproj_ref[0], rproj_ref[1]]
    back = [
        split(jnp.concatenate([place(m, half) for m in both], axis=0)) for half in range(2)
    ]

    def band_flux(g, carry):
        rows = pl.ds(pl.multiple_of(g * 128, 128), 128)
        left = [lside[rows, v * 128 : v * 128 + 128] for v in range(5)]
        right = [rside[rows, v * 128 : v * 128 + 128] for v in range(5)]
        flux = [split(x) for x in rusanov(left, right)]
        for t in range(3):
            y = dot3(dot_nn, flux[2 * t], back[0])
            if t < 2:
                y = y + dot3(dot_nn, flux[2 * t + 1], back[1])
            rflux[rows, t * 128 : t * 128 + 128] = y
        return carry

    lax.fori_loop(0, 3, band_flux, 0)
    ring(rflux, rflux_in, back_sem, my_rows)
    own_back = pltpu.make_async_copy(rflux.at[my_rows], rflux_in.at[my_rows], own_sem.at[6])
    own_back.start()

    code_rows = codes[...].T
    for chunk in range(2):
        own_chunk(chunk, lout, lin, own_sem.at[4 + chunk]).wait()
        wait_chunk(chunk, lin, l_sem)
        for pp in range(HALF):
            at = lambda v: pl.ds(chunk * CHUNK_ROWS + v * HALF + pp, ND, stride=MSG)
            slot = 2 * (chunk * HALF + pp)
            named = jnp.where(
                iota((ND, 128), 1) < FACE, codes[:, slot : slot + 1], codes[:, slot + 1 : slot + 2]
            )
            flux = rusanov([lin[at(v), :] for v in range(5)], [rout[at(v), :] for v in range(5)])
            for v in range(5):
                hi, lo = split(jnp.where(named > 0.5, flux[v], 0.0))
                fluxes_hi[pp * ND : pp * ND + ND, v * 128 : v * 128 + 128] = hi
                fluxes_lo[pp * ND : pp * ND + ND, v * 128 : v * 128 + 128] = lo
        for s in range(2):
            picks = []
            for par in range(2):
                pieces = []
                for pp in range(HALF):
                    slot = 2 * (chunk * HALF + pp) + par
                    line = code_rows[slot : slot + 1, :].astype(jnp.int32) - (1 + s * ELEMS)
                    pieces.append(hot(line == iota((ELEMS, ND), 0)))
                picks.append(jnp.concatenate(pieces, axis=1))
            for v in range(5):
                cols = slice(v * 128, v * 128 + 128)
                hi, lo = fluxes_hi[0 : HALF * ND, cols], fluxes_lo[0 : HALF * ND, cols]
                y = [dot_nn(x, hi) + dot_nn(x, lo) for x in picks]
                y = jnp.where(lower, y[0], y[1])
                rows = slice(s * ELEMS, s * ELEMS + ELEMS)
                if chunk == 0:
                    sums[rows, cols] = y
                else:
                    sums[rows, cols] += y

    def face_flux(src, node):
        at = lambda v: pl.ds(v * 512 + node, FACE, stride=8)
        result = [[] for _ in range(5)]
        for g in range(3):
            fields = [src[g, at(v), :] for v in range(5)]
            u, p, _ = primitive(fields)
            for v, value in enumerate(flux_along(fields, u[2], p, 2)):
                result[v].append(value)
        return [jnp.concatenate(r, axis=1) for r in result]

    adjoint = []
    for s in range(2):
        wide = jnp.concatenate([sproj_ref[s], jnp.zeros((FACE, FACE), F32)], axis=1)
        turned = jnp.concatenate([wide, wide], axis=0).T
        adjoint.append(split(turned[:FACE, :]))
    mine = face_flux(ss, 0)
    for v in range(5):
        cols = slice(v * 128, v * 128 + 128)
        y = dot3(dot_nt, adjoint[0], split(sums[0:ELEMS, cols]))
        y = y + dot3(dot_nt, adjoint[1], split(sums[ELEMS : 2 * ELEMS, cols]))
        ssurf[v * FACE : v * FACE + FACE, :] = (TIME_STEP * LIFT) * (0.5 * y - mine[v])

    own_back.wait()
    ring_wait(rflux_in, back_sem.at[1])
    mine = face_flux(rs, NODES - 1)
    for t in range(3):
        turned = jnp.concatenate(
            [rflux_in[g * 128 : g * 128 + 128, t * 128 : t * 128 + 128].T for g in range(3)], axis=1
        )
        for vh in range(2 if t < 2 else 1):
            v = 2 * t + vh
            y = turned[vh * FACE : vh * FACE + FACE, :]
            rsurf[v * FACE : v * FACE + FACE, :] = (-TIME_STEP * LIFT) * (0.5 * y - mine[v])

    for copy in stores:
        copy.wait()
    part = code_out.at[pl.ds(0, ND - 1)]
    pltpu.make_async_copy(part, part, code_sem.at[0]).wait()
    ring_wait(faces_r, trace_sem.at[0])
    ring_wait(rflux, back_sem.at[0])
    for chunk in range(4):
        rows = rout.at[pl.ds(0, (ND - 1) * MSG)]
        pltpu.make_async_copy(rows, rows, send_sem).wait()


def finish(rvol, svol, rsurf, ssurf, rnext, snext):
    for node, vol, surf, out in ((NODES - 1, rvol, rsurf, rnext), (0, svol, ssurf, snext)):
        at = pl.ds(node, FACE, stride=8)
        out[...] = vol[...]
        out[at, :] = vol[at, :] + surf[...]


def body(rotor_state, stator_state, rotor_projection, proj_stator, seg_owner, seg_row):
    vmem = pl.BlockSpec(memory_space=pltpu.VMEM)
    hbm = pl.BlockSpec(memory_space=pl.ANY)
    V = pltpu.VMEM
    dma = pltpu.SemaphoreType.DMA
    state = (ROWS, ELEMS)
    held = (3, ROWS, 128)
    big = jax.ShapeDtypeStruct(state, F32)
    small = jax.ShapeDtypeStruct((5 * FACE, ELEMS), F32)
    parts = pl.pallas_call(
        mega,
        out_shape=(big, big, small, small),
        in_specs=[vmem, vmem, vmem, vmem, hbm, hbm],
        out_specs=(hbm, hbm, vmem, vmem),
        scratch_shapes=[
            V(held, F32), V(held, F32), V(held, F32), V(held, F32),
            V((3 * 512, 128), F32), V((320, 128), F32), V((ROWS, 128), F32),
            V((ELEMS, 384), F32), V((ELEMS, 384), F32), V((ELEMS, 384), F32),
            V((ND, 1, 128), F32), V((ND, 1, 128), F32), V((ND, 128), F32), V((8, SEGS), F32),
            V((2 * SEGS, WIDE), BF16), V((2 * SEGS, WIDE), BF16),
            V((2 * SEGS, WIDE), BF16), V((2 * SEGS, WIDE), BF16),
            V((ELEMS, WIDE), F32), V((ELEMS, WIDE), F32), V((HALF * ND, 2 * SEGS), BF16),
            V((2 * CHUNK_ROWS, 128), F32), V((2 * CHUNK_ROWS, 128), F32),
            V((2 * CHUNK_ROWS, 128), F32), V((2 * CHUNK_ROWS, 128), F32),
            V((ELEMS, 384), F32), V((ELEMS, 384), F32),
            V((SEGS, WIDE), BF16), V((SEGS, WIDE), BF16), V((SEGS, WIDE), F32),
            dma((2, 3)), dma((2, 3)), dma((7,)), dma((2,)), dma((2,)), dma, dma((2,)), dma((2,)), dma((2,)),
        ],
        compiler_params=pltpu.CompilerParams(
            collective_id=0, has_side_effects=True, vmem_limit_bytes=56 * 2**20
        ),
    )(
        seg_owner.reshape(1, SEGS),
        seg_row.reshape(1, SEGS),
        rotor_projection,
        proj_stator,
        rotor_state.reshape(state),
        stator_state.reshape(state),
    )
    block = pl.BlockSpec((512, 128), lambda v, g: (v, g))
    face = pl.BlockSpec((FACE, 128), lambda v, g: (v, g))
    rotor_next, stator_next = pl.pallas_call(
        finish,
        grid=(5, 3),
        out_shape=(big, big),
        in_specs=[block, block, face, face],
        out_specs=(block, block),
        compiler_params=pltpu.CompilerParams(vmem_limit_bytes=32 * 2**20),
    )(*parts)
    return rotor_next.reshape(rotor_state.shape), stator_next.reshape(stator_state.shape)


def solution(mesh):
    spec = P(None, None, None, None, ("rotor", "stator"))
    in_specs = (spec, spec, P(), P(), P(("rotor", "stator"), None), P(("rotor", "stator")))
    return jax.shard_map(body, mesh=mesh, in_specs=in_specs, out_specs=(spec, spec), check_vma=False)
```

time: 340 us -> 106 us (0.31); the launches traced: 335 us -> 105 us
  local copies, waits for them, and re-layouts: 117 us -> 7.55 us
  other arithmetic: 101 us -> 0 us
  Pallas kernels: 0 us -> 97 us
  matrix products: 72.6 us -> 0 us
  starting transfers between devices: 42.9 us -> 0 us
    pallas_call x0 -> x2, Pallas kernels: none -> 97 us  [the longest x1 89.9 us: body(): pl.pallas_call(mega, out_shape=(big, big, small, small), in_specs=[vmem,...]
    dot_general x10 -> x0, matrix products: 72.6 us -> none  [the longest x6 53.7 us: volume_rate(): jnp.einsum(patterns[direction], matrix, flux_values, precision=TOP_PRECIS...]
    all_to_all x5 -> x0, starting transfers between devices: 42.9 us -> none  [the longest x1 11.1 us: body(): lax.all_to_all(outgoing_codes, ('rotor', 'stator'), split_axis=2, concat_...]
    all_to_all x3 -> x0, other arithmetic: 37.1 us -> none  [the longest x1 29.8 us: body(): lax.all_to_all(outgoing_codes, ('rotor', 'stator'), split_axis=2, concat_...]
    unnamed x70 -> x8, local copies, waits for them, and re-layouts: 35.8 us -> 6.28 us
    reshape x8 -> x1, local copies, waits for them, and re-layouts: 25.9 us -> 1.27 us  [body(): seg_row.reshape(1, SEGS)]
    scatter-add x3 -> x0, other arithmetic: 16.1 us -> none  [the longest x1 11.9 us: body(): stator_flux = jnp.zeros((row_width, elements), jnp.float32).at[:, row_ind...]
    unnamed x24 -> x0, other arithmetic: 15.5 us -> none
  transfers between devices with their start and end apart: 5 -> 0, of which waited for: 0 -> 0; matrix products, arithmetic and copies ran while one was open for 63% -> 0% of each run, Pallas kernels for 0% -> 0%
where the time goes in v1:
time: 106 us; the launch traced here: 105 us
  Pallas kernels  97 us (92%)
  local copies, waits for them, and re-layouts  7.55 us (7%)
    pallas_call x1, Pallas kernels, body(): pl.pallas_call(mega, out_shape=(big, big, small, small), in_specs=[vmem,...  89.9 us
    pallas_call x1, Pallas kernels, body(): pl.pallas_call(finish, grid=(5, 3), out_shape=(big, big), in_specs=[block...  7.1 us
    unnamed x8, local copies, waits for them, and re-layouts  6.28 us

profile of v1, /device:TPU:1, one launch (start us, length us, event | category | flops | bytes accessed | tf_op | source)
XLA Modules:
  0.0 105.2 jit_solution(10432751909311591525)
XLA Ops:
  0.6 1.3 %reshape.23.row_ref = s32[1,768]{1,0:T(1,128)} reshape(s32[768]{0:T(1024)} %param.11) | data formatting | bytes 6144 | tf_op jit(solution)/shard_map/reshape | solution.py:594
  1.9 89.9 %shard_map.77 = (f32[2560,384]{1,0:T(8,128)}, f32[2560,384]{1,0:T(8,128)}, f32[320,384]{1,0:T(8,128)}, f32[320,384]{1,0:T(8,128)}) custom-call(s32[1,768]{1,0:T(1,128)} %bitcast.7, s32[1,768]{1,0:T(1,128)} %reshape.23.row_ref, f32[2,64,64]{2,1,0:T(8,128)} %rproj_ref.1, f32[2,64,64]{2,1,0:T(8,128)} %sproj_ref.1, f32[2560,384]{1,0:T(8,128)} %bitcast.5, ...), custom_call_target="tpu_custom_call" | custom-call | tf_op jit(solution)/shard_map/pallas_call | solution.py:570
  91.8 0.0 copy-start
  91.8 2.1 %copy-done = f32[2560,384]{1,0:T(8,128)S(1)} copy-done((f32[2560,384]{1,0:T(8,128)S(1)}, f32[2560,384]{1,0:T(8,128)}, u32[]{:S(2)}) %copy-start) | copy-done | bytes 3932184
  93.9 0.0 copy-start.1
  93.9 2.1 %copy-done.1 = f32[2560,384]{1,0:T(8,128)S(1)} copy-done((f32[2560,384]{1,0:T(8,128)S(1)}, f32[2560,384]{1,0:T(8,128)}, u32[]{:S(2)}) %copy-start.1) | copy-done | bytes 3932184
  96.0 0.0 copy-start.2
  96.0 1.0 copy-done.2
  97.1 0.0 copy-start.3
  97.1 1.0 copy-done.3
  98.1 7.1 %shard_map.78 = (f32[2560,384]{1,0:T(8,128)}, f32[2560,384]{1,0:T(8,128)}) custom-call(f32[2560,384]{1,0:T(8,128)S(1)} %copy-done, f32[2560,384]{1,0:T(8,128)S(1)} %copy-done.1, f32[320,384]{1,0:T(8,128)S(1)} %copy-done.2, f32[320,384]{1,0:T(8,128)S(1)} %copy-done.3), custom_call_target="tpu_custom_call" | custom-call | tf_op jit(solution)/shard_map/pallas_call | solution.py:602
Async XLA Ops:
  91.8 2.1 %copy-start = (f32[2560,384]{1,0:T(8,128)S(1)}, f32[2560,384]{1,0:T(8,128)}, u32[]{:S(2)}) copy-start(f32[2560,384]{1,0:T(8,128)} %get-tuple-element.8.rvol) | copy-start | bytes 11796484
  93.9 2.1 %copy-start.1 = (f32[2560,384]{1,0:T(8,128)S(1)}, f32[2560,384]{1,0:T(8,128)}, u32[]{:S(2)}) copy-start(f32[2560,384]{1,0:T(8,128)} %get-tuple-element.9.svol) | copy-start | bytes 11796484
  96.0 1.0 copy-start.2
  97.1 1.0 copy-start.3

commit v2 on v1

v2 whole, which is shorter than its diff:
```python
import functools

import jax
import jax.numpy as jnp
import numpy as np
from jax import lax
from jax.experimental import pallas as pl
from jax.experimental.pallas import tpu as pltpu
from jax.sharding import PartitionSpec as P

NODES = 8
FACE = 64
NR = 8
NS = 16
ND = NR * NS
ELEMS = 384
BAND = ELEMS // NR
SEGS = 2 * ELEMS
ROWS = 5 * NODES * FACE
CAP = 12
PAIRS = CAP // 2
HALF = PAIRS // 2
MSG = 16
SENT = 15
CHUNK_ROWS = ND * MSG
WIDE = 5 * 128
GAMMA = 1.4
TIME_STEP = 0.02
LIFT = 28.0
MESH = pl.DeviceIdType.MESH
F32 = jnp.float32
BF16 = jnp.bfloat16


def cheb_matrix():
    degree = NODES - 1
    j = np.arange(degree + 1)
    points = -np.cos(np.pi * j / degree)
    weights = np.where((j == 0) | (j == degree), 2.0, 1.0) * (-1.0) ** j
    spacing = points[:, None] - points[None, :]
    identity = np.eye(degree + 1)
    matrix = weights[:, None] / weights[None, :] / (spacing + identity)
    matrix = matrix - identity * matrix.sum(axis=1)[:, None]
    return matrix.astype(np.float32)


DM = cheb_matrix().astype(np.float64) * (-TIME_STEP * 0.5)
ODD = DM[:4, :4] - DM[:4, :3:-1]
EVEN = DM[:4, :4] + DM[:4, :3:-1]


def derive(line):
    plus = [line[j] + line[7 - j] for j in range(4)]
    minus = [line[j] - line[7 - j] for j in range(4)]
    out = [None] * 8
    for i in range(4):
        p = sum(float(ODD[i, j]) * minus[j] for j in range(4))
        q = sum(float(EVEN[i, j]) * plus[j] for j in range(4))
        out[i] = p + q
        out[7 - i] = p - q
    return out


def primitive(fields):
    density, mx, my, mz, energy = fields
    inverse = 1.0 / density
    u = (mx * inverse, my * inverse, mz * inverse)
    kinetic = mx * u[0] + my * u[1] + mz * u[2]
    return u, (GAMMA - 1.0) * (energy - 0.5 * kinetic), inverse


def flux_along(fields, speed, pressure, direction):
    result = [fields[1 + direction]]
    for k in range(3):
        term = fields[1 + k] * speed
        result.append(term + pressure if k == direction else term)
    result.append((fields[4] + pressure) * speed)
    return result


def rusanov(left, right):
    lu, lp, li = primitive(left)
    ru, rp, ri = primitive(right)
    lf = flux_along(left, lu[2], lp, 2)
    rf = flux_along(right, ru[2], rp, 2)
    signal = jnp.maximum(
        jnp.abs(lu[2]) + jnp.sqrt(GAMMA * lp * li), jnp.abs(ru[2]) + jnp.sqrt(GAMMA * rp * ri)
    )
    return [
        0.5 * (lf[v] + rf[v]) - 0.5 * signal * (right[v] - left[v]) for v in range(5)
    ]


def split(x):
    hi = x.astype(BF16)
    return hi, (x - hi.astype(F32)).astype(BF16)


def dot_nn(a, b):
    return lax.dot_general(a, b, (((1,), (0,)), ((), ())), preferred_element_type=F32)


def dot_nt(a, b):
    return lax.dot_general(a, b, (((1,), (1,)), ((), ())), preferred_element_type=F32)


def dot3(dot, a, b):
    return dot(a[0], b[0]) + dot(a[0], b[1]) + dot(a[1], b[0])


def hot(mask):
    return jnp.where(mask, 1.0, 0.0).astype(BF16)


def iota(shape, dim):
    return lax.broadcasted_iota(jnp.int32, shape, dim)


def volume_first(src, prim, tmp, acc, step):
    t, a = lax.div(step, 8), lax.rem(step, 8)
    at = lambda v, b: pl.ds(pl.multiple_of(v * 512 + a * 64 + b * 8, 8), 8)
    lines = [[] for _ in range(5)]
    for b in range(8):
        fields = [src[t, at(v, b), :] for v in range(5)]
        u, p, _ = primitive(fields)
        prim[at(0, b), :] = u[0]
        prim[at(1, b), :] = u[2]
        prim[at(2, b), :] = p
        for v, value in enumerate(flux_along(fields, u[1], p, 1)):
            lines[v].append(value)
    for v in range(5):
        for b, value in enumerate(derive(lines[v])):
            acc[at(v, b), :] = value
    column = lambda v, c: pl.ds(v * 512 + a * 64 + c, 8, stride=8)
    lines = [[] for _ in range(5)]
    for c in range(8):
        fields = [None] + [src[t, column(v, c), :] for v in range(1, 5)]
        for v, value in enumerate(
            flux_along(fields, prim[column(1, c), :], prim[column(2, c), :], 2)
        ):
            lines[v].append(value)
    for v in range(5):
        for c, value in enumerate(derive(lines[v])):
            tmp[pl.ds(v * 64 + c, 8, stride=8), :] = value
    for v in range(5):
        for b in range(8):
            acc[at(v, b), :] += tmp[v * 64 + b * 8 : v * 64 + b * 8 + 8, :]


def volume_second(src, prim, acc, out, t, b):
    at = lambda v, a: pl.ds(pl.multiple_of(v * 512 + a * 64 + b * 8, 8), 8)
    lines = [[] for _ in range(5)]
    for a in range(8):
        fields = [None] + [src[t, at(v, a), :] for v in range(1, 5)]
        for v, value in enumerate(
            flux_along(fields, prim[at(0, a), :], prim[at(2, a), :], 0)
        ):
            lines[v].append(value)
    for v in range(5):
        for a, value in enumerate(derive(lines[v])):
            out[t, at(v, a), :] = src[t, at(v, a), :] + (acc[at(v, a), :] + value)


def volume(src, out, prim, tmp, acc, tiles):
    for t in tiles:

        def first(a, carry):
            volume_first(src, prim, tmp, acc, t * 8 + a)
            return carry

        def second(b, carry):
            volume_second(src, prim, acc, out, t, b)
            return carry

        lax.fori_loop(0, 8, first, 0)
        lax.fori_loop(0, 8, second, 0)


def face_rows(src, node, dst):
    for t in range(3):
        count = 128 if t < 2 else 64
        rows = [
            src[g, pl.ds(t * 1024 + node, count, stride=8), :]
            for g in range(3)
        ]
        for g in range(3):
            block = rows[g]
            if t == 2:
                block = jnp.concatenate([block, jnp.zeros((64, 128), F32)], axis=0)
            dst[g * 128 : g * 128 + 128, t * 128 : t * 128 + 128] = block.T


def pair(a, b):
    lower = iota(a.shape, 1) < FACE
    return (
        jnp.where(lower, a, pltpu.roll(b, FACE, 1)),
        jnp.where(lower, pltpu.roll(a, FACE, 1), b),
    )


def diagonal(matrix):
    zero = jnp.zeros((FACE, FACE), F32)
    top = jnp.concatenate([matrix, zero], axis=1)
    bottom = jnp.concatenate([zero, matrix], axis=1)
    return jnp.concatenate([top, bottom], axis=0)


def lanes_of(t):
    return (t * 128, 256 + t * 128) if t < 2 else (512, 640)


def put_parts(ref, rows, t, x):
    for start, piece in zip(lanes_of(t), split(x)):
        ref[rows, start : start + 128] = piece


def pick(hots, table):
    y = dot_nn(hots, table[:, 0:256]) + dot_nn(hots, table[:, 256:512])
    z = dot_nn(hots, table[:, 512:768])
    return y, z[:, :128] + z[:, 128:]


def make_table(faces, proj, table, side_ref):
    hi, lo = split(jnp.concatenate([diagonal(proj[0]), diagonal(proj[1])], axis=0))
    both = jnp.concatenate([hi, lo], axis=1)

    def body(g, carry):
        rows = pl.ds(pl.multiple_of(g * 128, 128), 128)
        for t in range(3):
            x, rest = split(faces[rows, t * 128 : t * 128 + 128])
            y = dot_nt(jnp.concatenate([x, x], axis=1), both) + dot_nt(rest, hi)
            sides = (y[:, :128], y[:, 128:])
            for s in range(2):
                at = pl.ds(pl.multiple_of(s * ELEMS + g * 128, 128), 128)
                put_parts(table, at, t, sides[s])
            if side_ref is not None:
                first, second = pair(*sides)
                side_ref[rows, 2 * t * 128 : 2 * t * 128 + 128] = first
                if t < 2:
                    side_ref[rows, 2 * t * 128 + 128 : 2 * t * 128 + 256] = second
        return carry

    lax.fori_loop(0, 3, body, 0)


def message_row(chunk, row):
    return pl.ds(chunk * CHUNK_ROWS + row, ND, stride=MSG)


def gather_chunk(chunk, hots, table, message):
    y, z = pick(hots[...], table)
    lower = iota((ND, 128), 1) < FACE
    for r in range(PAIRS):
        rows = slice(r * ND, r * ND + ND)
        for t in range(2):
            message[message_row(chunk, 2 * r + t), :] = y[rows, t * 128 : t * 128 + 128]
    for pp in range(HALF):
        even = z[2 * pp * ND : 2 * pp * ND + ND, :]
        odd = z[2 * pp * ND + ND : 2 * pp * ND + 2 * ND, :]
        message[message_row(chunk, 12 + pp), :] = jnp.where(lower, even, pltpu.roll(odd, FACE, 1))


def mega(
    owner_ref, row_ref, rproj_ref, sproj_ref, rstate, sstate,
    ru, su,
    rs, ss, prim, tmp, acc,
    faces_s, faces_r, bands, code_out, code_in, codes, seg,
    tab, ltab, lside, rside, hots, seg_hots, sum_hots,
    rout, rin, lout, lin, rflux, rflux_in, arrived, sums,
    load_sem, own_sem, code_sem, trace_sem, send_sem, r_sem, l_sem, back_sem,
):
    mi, mj = lax.axis_index("rotor"), lax.axis_index("stator")
    me = mi * NS + mj
    tiles = lambda ref, t: ref.at[:, pl.ds(t * 128, 128)]
    loads = [
        [
            pltpu.make_async_copy(tiles(state, t), held.at[t], load_sem.at[n, t])
            for t in range(3)
        ]
        for n, (state, held) in enumerate(((rstate, rs), (sstate, ss)))
    ]
    for copy in loads[0] + loads[1]:
        copy.start()

    def coords(d):
        return (lax.div(d, NS), lax.rem(d, NS))

    def peer(p):
        o = lax.rem(p * 37, ND)
        return lax.rem(lax.div(o, NS) + mi, NR), lax.rem(lax.rem(o, NS) + mj, NS)

    barrier = pltpu.get_barrier_semaphore()

    def greet(p, carry):
        pl.semaphore_signal(
            barrier, inc=1, device_id=coords(lax.rem(me + p, ND)), device_id_type=MESH
        )
        return carry

    lax.fori_loop(1, ND, greet, 0)

    owner = owner_ref[...].astype(F32)
    code = row_ref[...]
    lane = iota((1, SEGS), 1)
    side = lax.rem(lane, 2)
    code = code + side * ELEMS + 1
    high = lax.div(code, 4).astype(F32)
    low = lax.rem(code, 4).astype(F32)
    packed = jnp.concatenate([owner, high, low, jnp.zeros((5, SEGS), F32)], axis=0).astype(BF16)
    new = iota((SEGS, SEGS), 0)
    old = iota((SEGS, SEGS), 1)
    order = hot(old == jnp.where(new < ELEMS, 2 * new, 2 * new - 2 * ELEMS + 1))
    by_side = dot_nt(packed, order)
    owner = by_side[0:1]
    member = owner == iota((ND, SEGS), 0).astype(F32)
    member_hot = hot(member)
    earlier = dot_nn(member_hot, hot(new < old))
    rank = jnp.sum(jnp.where(member, earlier, 0.0), axis=0, keepdims=True)
    seg[0:1, :] = owner
    seg[1:2, :] = rank
    seg[2:8, :] = jnp.zeros((6, SEGS), F32)
    ranked = rank == iota((ND, SEGS), 0).astype(F32)
    table = 4.0 * dot_nt(member_hot, jnp.where(ranked, by_side[1:2], 0.0).astype(BF16))
    table = table + dot_nt(member_hot, jnp.where(ranked, by_side[2:3], 0.0).astype(BF16))
    code_out[...] = table.reshape(ND, 1, 128)

    for copy in loads[0]:
        copy.wait()
    face_rows(rs, NODES - 1, faces_r)
    for copy in loads[1]:
        copy.wait()
    face_rows(ss, 0, faces_s)
    make_table(faces_s, sproj_ref, tab, None)

    pl.semaphore_wait(barrier, ND - 1)

    def ring(src, dst, sems, me_rows):
        def send(p, carry):
            i = lax.rem(mi + p, NR)
            pltpu.make_async_remote_copy(
                src_ref=src.at[pl.ds(pl.multiple_of(i * BAND, 16), BAND)],
                dst_ref=dst.at[me_rows],
                send_sem=sems.at[0], recv_sem=sems.at[1],
                device_id=(i, mj), device_id_type=MESH,
            ).start()
            return carry

        lax.fori_loop(1, NR, send, 0)

    def ring_wait(dst, sem):
        rows = dst.at[pl.ds(0, (NR - 1) * BAND)]
        pltpu.make_async_copy(rows, rows, sem).wait()

    my_rows = pl.ds(pl.multiple_of(mi * BAND, 16), BAND)
    ring(faces_r, bands, trace_sem, my_rows)
    def send_code(p, carry):
        i, j = peer(p)
        pltpu.make_async_remote_copy(
            src_ref=code_out.at[i * NS + j], dst_ref=code_in.at[me],
            send_sem=code_sem.at[0], recv_sem=code_sem.at[1],
            device_id=(i, j), device_id_type=MESH,
        ).start()
        return carry

    lax.fori_loop(1, ND, send_code, 0)
    own = pltpu.make_async_copy(code_out.at[me], code_in.at[me], own_sem.at[0])
    own.start()
    own_trace = pltpu.make_async_copy(faces_r.at[my_rows], bands.at[my_rows], own_sem.at[1])
    own_trace.start()

    volume(rs, ru, prim, tmp, acc, range(2))

    own.wait()
    part = code_in.at[pl.ds(0, ND - 1)]
    pltpu.make_async_copy(part, part, code_sem.at[1]).wait()
    codes[...] = code_in[...].reshape(ND, 128)

    def send_chunk(chunk, src, dst, sems):
        def send(p, carry):
            i, j = peer(p)
            at = pl.ds(pl.multiple_of(chunk * CHUNK_ROWS + (i * NS + j) * MSG, MSG), SENT)
            to = pl.ds(pl.multiple_of(chunk * CHUNK_ROWS + me * MSG, MSG), SENT)
            pltpu.make_async_remote_copy(
                src_ref=src.at[at], dst_ref=dst.at[to],
                send_sem=send_sem, recv_sem=sems.at[chunk],
                device_id=(i, j), device_id_type=MESH,
            ).start()
            return carry

        lax.fori_loop(1, ND, send, 0)

    def wait_chunk(chunk, dst, sems):
        rows = dst.at[pl.ds(chunk * CHUNK_ROWS, (ND - 1) * SENT)]
        pltpu.make_async_copy(rows, rows, sems.at[chunk]).wait()

    def own_chunk(chunk, src, dst, sem):
        to = pl.ds(pl.multiple_of(chunk * CHUNK_ROWS + me * MSG, MSG), SENT)
        return pltpu.make_async_copy(src.at[to], dst.at[to], sem)

    for chunk in range(2):
        for r in range(PAIRS):
            slot = chunk * PAIRS + r
            column = codes[:, slot : slot + 1].astype(jnp.int32) - 1
            hots[r * ND : r * ND + ND, :] = hot(column == iota((ND, SEGS), 1))
        gather_chunk(chunk, hots, tab, rout)
        send_chunk(chunk, rout, rin, r_sem)
        own_chunk(chunk, rout, rin, own_sem.at[2 + chunk]).start()

    own_trace.wait()
    ring_wait(bands, trace_sem.at[1])
    make_table(bands, rproj_ref, ltab, lside)
    for chunk in range(2):
        belongs = seg[0:1, :] == iota((ND, SEGS), 0).astype(F32)
        for r in range(PAIRS):
            slot = chunk * PAIRS + r
            hots[r * ND : r * ND + ND, :] = hot(
                jnp.logical_and(belongs, seg[1:2, :] == float(slot))
            )
        gather_chunk(chunk, hots, ltab, lout)
        send_chunk(chunk, lout, lin, l_sem)
        own_chunk(chunk, lout, lin, own_sem.at[4 + chunk]).start()

    columns = seg[...].T.astype(jnp.int32)
    code_rows = codes[...].T.astype(jnp.int32)
    for s in range(2):
        rows = slice(s * ELEMS, s * ELEMS + ELEMS)
        slot = columns[rows, 1:2] * ND + columns[rows, 0:1]
        for r in range(CAP):
            cols = slice(r * ND, r * ND + ND)
            seg_hots[rows, cols] = hot(slot == iota((ELEMS, ND), 1) + r * ND)
            line = code_rows[r : r + 1, :] - (1 + s * ELEMS)
            sum_hots[rows, cols] = hot(line == iota((ELEMS, ND), 0))
    volume(rs, ru, prim, tmp, acc, range(2, 3))
    volume(ss, su, prim, tmp, acc, range(3))

    lower = iota((ND, 128), 1) < FACE
    for chunk in range(2):
        own_chunk(chunk, rout, rin, own_sem.at[2 + chunk]).wait()
        wait_chunk(chunk, rin, r_sem)
        for r in range(PAIRS):
            at = pl.ds((chunk * PAIRS + r) * ND, ND)
            for t in range(2):
                put_parts(arrived, at, t, rin[message_row(chunk, 2 * r + t), :])
            x = rin[message_row(chunk, 12 + r // 2), :]
            if r % 2:
                x = pltpu.roll(x, FACE, 1)
            put_parts(arrived, at, 2, jnp.where(lower, x, 0.0))
    for s in range(2):
        rows = slice(s * ELEMS, s * ELEMS + ELEMS)
        y, z = pick(seg_hots[rows, :], arrived)
        rside[rows, 0:256] = y
        rside[rows, 256:384] = z
    zero = jnp.zeros((FACE, FACE), F32)
    back = []
    for half in range(2):
        blocks = [
            jnp.concatenate([rproj_ref[s], zero] if half == 0 else [zero, rproj_ref[s]], axis=1)
            for s in range(2)
        ]
        back.append(split(jnp.concatenate(blocks, axis=0)))

    def band_flux(g, carry):
        rows = pl.ds(pl.multiple_of(g * 128, 128), 128)
        others = pl.ds(pl.multiple_of(ELEMS + g * 128, 128), 128)
        left = [lside[rows, v * 128 : v * 128 + 128] for v in range(5)]
        right = []
        for t in range(3):
            cols = slice(t * 128, t * 128 + 128)
            right += list(pair(rside[rows, cols], rside[others, cols]))
        flux = [split(x) for x in rusanov(left, right[:5])]
        for t in range(3):
            y = dot3(dot_nn, flux[2 * t], back[0])
            if t < 2:
                y = y + dot3(dot_nn, flux[2 * t + 1], back[1])
            rflux[rows, t * 128 : t * 128 + 128] = y
        return carry

    lax.fori_loop(0, 3, band_flux, 0)
    ring(rflux, rflux_in, back_sem, my_rows)
    own_back = pltpu.make_async_copy(rflux.at[my_rows], rflux_in.at[my_rows], own_sem.at[6])
    own_back.start()

    def fields(ref, chunk, pp):
        tile = lambda r, t: ref[message_row(chunk, 2 * (2 * pp + r) + t), :]
        return [
            *pair(tile(0, 0), tile(1, 0)),
            *pair(tile(0, 1), tile(1, 1)),
            ref[message_row(chunk, 12 + pp), :],
        ]

    for chunk in range(2):
        own_chunk(chunk, lout, lin, own_sem.at[4 + chunk]).wait()
        wait_chunk(chunk, lin, l_sem)
        for pp in range(HALF):
            slot = chunk * PAIRS + 2 * pp
            named = jnp.where(lower, codes[:, slot : slot + 1], codes[:, slot + 1 : slot + 2])
            flux = [
                jnp.where(named > 0.5, x, 0.0)
                for x in rusanov(fields(lin, chunk, pp), fields(rout, chunk, pp))
            ]
            first = [*pair(flux[0], flux[1])], [*pair(flux[2], flux[3])]
            last = (
                jnp.where(lower, flux[4], 0.0),
                jnp.where(lower, pltpu.roll(flux[4], FACE, 1), 0.0),
            )
            for r in range(2):
                at = pl.ds((2 * pp + r) * ND, ND)
                put_parts(arrived, at, 0, first[0][r])
                put_parts(arrived, at, 1, first[1][r])
                put_parts(arrived, at, 2, last[r])
        for s in range(2):
            rows = slice(s * ELEMS, s * ELEMS + ELEMS)
            some = sum_hots[rows, chunk * PAIRS * ND : (chunk + 1) * PAIRS * ND]
            y, z = pick(some, arrived.at[pl.ds(0, PAIRS * ND)])
            if chunk == 0:
                sums[rows, 0:256] = y
                sums[rows, 256:384] = z
            else:
                sums[rows, 0:256] += y
                sums[rows, 256:384] += z

    def face_flux(src, node):
        at = lambda v: pl.ds(v * 512 + node, FACE, stride=8)
        result = [[] for _ in range(5)]
        for g in range(3):
            fields = [src[g, at(v), :] for v in range(5)]
            u, p, _ = primitive(fields)
            for v, value in enumerate(flux_along(fields, u[2], p, 2)):
                result[v].append(value)
        return [jnp.concatenate(r, axis=1) for r in result]

    def add(out, node, v, change):
        for g in range(3):
            at = pl.ds(v * 512 + node, FACE, stride=8)
            out[g, at, :] = out[g, at, :] + change[:, g * 128 : g * 128 + 128]

    adjoint = jnp.concatenate([diagonal(sproj_ref[0]), diagonal(sproj_ref[1])], axis=0)
    adjoint = split(adjoint.T)
    mine = face_flux(ss, 0)
    for t in range(3):
        cols = slice(t * 128, t * 128 + 128)
        both = jnp.concatenate([sums[0:ELEMS, cols], sums[ELEMS : 2 * ELEMS, cols]], axis=1)
        y = dot3(dot_nt, adjoint, split(both))
        for vh in range(2 if t < 2 else 1):
            v = 2 * t + vh
            flux = 0.5 * y[vh * FACE : vh * FACE + FACE, :]
            add(su, 0, v, (TIME_STEP * LIFT) * (flux - mine[v]))

    own_back.wait()
    ring_wait(rflux_in, back_sem.at[1])
    mine = face_flux(rs, NODES - 1)
    for t in range(3):
        turned = jnp.concatenate(
            [rflux_in[g * 128 : g * 128 + 128, t * 128 : t * 128 + 128].T for g in range(3)], axis=1
        )
        for vh in range(2 if t < 2 else 1):
            v = 2 * t + vh
            y = turned[vh * FACE : vh * FACE + FACE, :]
            add(ru, NODES - 1, v, (-TIME_STEP * LIFT) * (0.5 * y - mine[v]))

    part = code_out.at[pl.ds(0, ND - 1)]
    pltpu.make_async_copy(part, part, code_sem.at[0]).wait()
    ring_wait(faces_r, trace_sem.at[0])
    ring_wait(rflux, back_sem.at[0])
    for chunk in range(4):
        rows = rout.at[pl.ds(0, (ND - 1) * SENT)]
        pltpu.make_async_copy(rows, rows, send_sem).wait()


def finish(ru, su, rnext, snext, sem):
    copies = [
        pltpu.make_async_copy(held.at[t], out.at[:, pl.ds(t * 128, 128)], sem.at[n, t])
        for n, (held, out) in enumerate(((ru, rnext), (su, snext)))
        for t in range(3)
    ]
    for copy in copies:
        copy.start()
    for copy in copies:
        copy.wait()


def body(rotor_state, stator_state, rotor_projection, proj_stator, seg_owner, seg_row):
    vmem = pl.BlockSpec(memory_space=pltpu.VMEM)
    hbm = pl.BlockSpec(memory_space=pl.ANY)
    V = pltpu.VMEM
    dma = pltpu.SemaphoreType.DMA
    state = (ROWS, ELEMS)
    held = (3, ROWS, 128)
    big = jax.ShapeDtypeStruct(state, F32)
    parts = pl.pallas_call(
        mega,
        out_shape=(V(held, F32), V(held, F32)),
        in_specs=[vmem, vmem, vmem, vmem, hbm, hbm],
        scratch_shapes=[
            V(held, F32), V(held, F32),
            V((3 * 512, 128), F32), V((320, 128), F32), V((ROWS, 128), F32),
            V((ELEMS, 384), F32), V((ELEMS, 384), F32), V((ELEMS, 384), F32),
            V((ND, 1, 128), F32), V((ND, 1, 128), F32), V((ND, 128), F32), V((8, SEGS), F32),
            V((SEGS, SEGS), BF16), V((SEGS, SEGS), BF16), V((ELEMS, WIDE), F32), V((SEGS, 384), F32),
            V((PAIRS * ND, SEGS), BF16), V((SEGS, CAP * ND), BF16), V((SEGS, CAP * ND), BF16),
            V((2 * CHUNK_ROWS, 128), F32), V((2 * CHUNK_ROWS, 128), F32),
            V((2 * CHUNK_ROWS, 128), F32), V((2 * CHUNK_ROWS, 128), F32),
            V((ELEMS, 384), F32), V((ELEMS, 384), F32),
            V((CAP * ND, SEGS), BF16), V((SEGS, 384), F32),
            dma((2, 3)), dma((7,)), dma((2,)), dma((2,)), dma, dma((2,)), dma((2,)), dma((2,)),
        ],
        compiler_params=pltpu.CompilerParams(
            collective_id=0, has_side_effects=True, vmem_limit_bytes=48 * 2**20
        ),
    )(
        seg_owner.reshape(1, SEGS),
        seg_row.reshape(1, SEGS),
        rotor_projection,
        proj_stator,
        rotor_state.reshape(state),
        stator_state.reshape(state),
    )
    rotor_next, stator_next = pl.pallas_call(
        finish,
        out_shape=(big, big),
        in_specs=[hbm, hbm],
        out_specs=(hbm, hbm),
        scratch_shapes=[dma((2, 3))],
        compiler_params=pltpu.CompilerParams(vmem_limit_bytes=4 * 2**20),
    )(*parts)
    return rotor_next.reshape(rotor_state.shape), stator_next.reshape(stator_state.shape)


def solution(mesh):
    spec = P(None, None, None, None, ("rotor", "stator"))
    in_specs = (spec, spec, P(), P(), P(("rotor", "stator"), None), P(("rotor", "stator")))
    return jax.shard_map(body, mesh=mesh, in_specs=in_specs, out_specs=(spec, spec), check_vma=False)
```

time: 106 us -> 81.3 us (0.77)
  Pallas kernels: 97 us -> 79.1 us
  local copies, waits for them, and re-layouts: 7.55 us -> 1.27 us
    pallas_call x2, Pallas kernels: 97 us -> 79.1 us  [the longest x1 75.9 us: body(): pl.pallas_call(mega, out_shape=(V(held, F32), V(held, F32)), in_specs=[vm...]
    unnamed x8 -> x0, local copies, waits for them, and re-layouts: 6.28 us -> none
where the time goes in v2:
time: 81.3 us; the launch traced here: 81.2 us
  Pallas kernels  79.1 us (97%)
  local copies, waits for them, and re-layouts  1.27 us (2%)
    pallas_call x1, Pallas kernels, body(): pl.pallas_call(mega, out_shape=(V(held, F32), V(held, F32)), in_specs=[vm...  75.9 us
    pallas_call x1, Pallas kernels, body(): pl.pallas_call(finish, out_shape=(big, big), in_specs=[hbm, hbm], out_spe...  3.23 us

profile of v2, /device:TPU:1, one launch (start us, length us, event | category | flops | bytes accessed | tf_op | source)
XLA Modules:
  0.0 81.2 jit_solution(6319118168563329229)
XLA Ops:
  0.6 1.3 %reshape.23.row_ref = s32[1,768]{1,0:T(1,128)} reshape(s32[768]{0:T(1024)} %param.11) | data formatting | bytes 6144 | tf_op jit(solution)/shard_map/reshape | solution.py:612
  1.9 75.9 %shard_map.77 = (f32[3,2560,128]{2,1,0:T(8,128)S(1)}, f32[3,2560,128]{2,1,0:T(8,128)S(1)}) custom-call(s32[1,768]{1,0:T(1,128)} %bitcast.7, s32[1,768]{1,0:T(1,128)} %reshape.23.row_ref, f32[2,64,64]{2,1,0:T(8,128)} %rproj_ref.1, f32[2,64,64]{2,1,0:T(8,128)} %sproj_ref.1, f32[2560,384]{1,0:T(8,128)} %bitcast.5, f32[2560,384]{1,0:T(8,128)} %bitcast.6), custom_call_target="tpu_custom_call" | custom-call | tf_op jit(solution)/shard_map/pallas_call | solution.py:590
  77.8 3.2 %shard_map.78 = (f32[2560,384]{1,0:T(8,128)}, f32[2560,384]{1,0:T(8,128)}) custom-call(f32[3,2560,128]{2,1,0:T(8,128)S(1)} %get-tuple-element.6.ru, f32[3,2560,128]{2,1,0:T(8,128)S(1)} %get-tuple-element.7.su), custom_call_target="tpu_custom_call" | custom-call | tf_op jit(solution)/shard_map/pallas_call | solution.py:618

commit v3 on v2

--- a/solution.py
+++ b/solution.py
@@ -243,6 +243,26 @@
     lax.fori_loop(0, 3, body, 0)
 
 
+def pack_last(faces, packed):
+    lower = iota((BAND // 2, 128), 1) < FACE
+    for i in range(NR):
+        first = faces[i * BAND : i * BAND + BAND // 2, 256:384]
+        second = faces[i * BAND + BAND // 2 : i * BAND + BAND, 256:384]
+        packed[i * BAND // 2 : (i + 1) * BAND // 2, :] = jnp.where(
+            lower, first, pltpu.roll(second, FACE, 1)
+        )
+
+
+def unpack_last(packed, faces):
+    lower = iota((BAND // 2, 128), 1) < FACE
+    for i in range(NR):
+        x = packed[i * BAND // 2 : (i + 1) * BAND // 2, :]
+        faces[i * BAND : i * BAND + BAND // 2, 256:384] = jnp.where(lower, x, 0.0)
+        faces[i * BAND + BAND // 2 : i * BAND + BAND, 256:384] = jnp.where(
+            lower, pltpu.roll(x, FACE, 1), 0.0
+        )
+
+
 def message_row(chunk, row):
     return pl.ds(chunk * CHUNK_ROWS + row, ND, stride=MSG)
 
@@ -266,7 +286,7 @@
     rs, ss, prim, tmp, acc,
     faces_s, faces_r, bands, code_out, code_in, codes, seg,
     tab, ltab, lside, rside, hots, seg_hots, sum_hots,
-    rout, rin, lout, lin, rflux, rflux_in, arrived, sums,
+    rout, rin, lout, lin, rflux, rflux_in, last_out, last_in, last_back, arrived, sums,
     load_sem, own_sem, code_sem, trace_sem, send_sem, r_sem, l_sem, back_sem,
 ):
     mi, mj = lax.axis_index("rotor"), lax.axis_index("stator")
@@ -300,7 +320,7 @@
     lax.fori_loop(1, ND, greet, 0)
 
     owner = owner_ref[...].astype(F32)
-    code = row_ref[...]
+    code = row_ref[...].reshape(1, SEGS)
     lane = iota((1, SEGS), 1)
     side = lax.rem(lane, 2)
     code = code + side * ELEMS + 1
@@ -327,6 +347,7 @@
     for copy in loads[0]:
         copy.wait()
     face_rows(rs, NODES - 1, faces_r)
+    pack_last(faces_r, last_out)
     for copy in loads[1]:
         copy.wait()
     face_rows(ss, 0, faces_s)
@@ -334,25 +355,29 @@
 
     pl.semaphore_wait(barrier, ND - 1)
 
-    def ring(src, dst, sems, me_rows):
-        def send(p, carry):
-            i = lax.rem(mi + p, NR)
+    block = lambda ref, i: ref.at[pl.ds(pl.multiple_of(i * BAND, 16), BAND), pl.ds(0, 256)]
+    tail_block = lambda ref, i: ref.at[pl.ds(pl.multiple_of(i * BAND // 2, 8), BAND // 2)]
+
+    def ring_send(i, src, dst, src_last, dst_last, sems):
+        for n, (cut, a, b) in enumerate(((block, src, dst), (tail_block, src_last, dst_last))):
             pltpu.make_async_remote_copy(
-                src_ref=src.at[pl.ds(pl.multiple_of(i * BAND, 16), BAND)],
-                dst_ref=dst.at[me_rows],
-                send_sem=sems.at[0], recv_sem=sems.at[1],
+                src_ref=cut(a, i), dst_ref=cut(b, mi),
+                send_sem=sems.at[0, n], recv_sem=sems.at[1, n],
                 device_id=(i, mj), device_id_type=MESH,
             ).start()
-            return carry
-
-        lax.fori_loop(1, NR, send, 0)
-
-    def ring_wait(dst, sem):
-        rows = dst.at[pl.ds(0, (NR - 1) * BAND)]
-        pltpu.make_async_copy(rows, rows, sem).wait()
-
-    my_rows = pl.ds(pl.multiple_of(mi * BAND, 16), BAND)
-    ring(faces_r, bands, trace_sem, my_rows)
+
+    def ring_wait(dst, dst_last, sems, side):
+        rows = dst.at[pl.ds(0, (NR - 1) * BAND), pl.ds(0, 256)]
+        pltpu.make_async_copy(rows, rows, sems.at[side, 0]).wait()
+        rows = dst_last.at[pl.ds(0, (NR - 1) * BAND // 2)]
+        pltpu.make_async_copy(rows, rows, sems.at[side, 1]).wait()
+
+    def ring_own(src, dst, src_last, dst_last, n):
+        return [
+            pltpu.make_async_copy(block(src, mi), block(dst, mi), own_sem.at[n]),
+            pltpu.make_async_copy(tail_block(src_last, mi), tail_block(dst_last, mi), own_sem.at[n + 1]),
+        ]
+
     def send_code(p, carry):
         i, j = peer(p)
         pltpu.make_async_remote_copy(
@@ -362,11 +387,17 @@
         ).start()
         return carry
 
+    def send_trace(p, carry):
+        ring_send(lax.rem(mi + p, NR), faces_r, bands, last_out, last_in, trace_sem)
+        return carry
+
     lax.fori_loop(1, ND, send_code, 0)
+    lax.fori_loop(1, NR, send_trace, 0)
     own = pltpu.make_async_copy(code_out.at[me], code_in.at[me], own_sem.at[0])
     own.start()
-    own_trace = pltpu.make_async_copy(faces_r.at[my_rows], bands.at[my_rows], own_sem.at[1])
-    own_trace.start()
+    own_trace = ring_own(faces_r, bands, last_out, last_in, 6)
+    for copy in own_trace:
+        copy.start()
 
     volume(rs, ru, prim, tmp, acc, range(2))
 
@@ -406,8 +437,10 @@
         send_chunk(chunk, rout, rin, r_sem)
         own_chunk(chunk, rout, rin, own_sem.at[2 + chunk]).start()
 
-    own_trace.wait()
-    ring_wait(bands, trace_sem.at[1])
+    for copy in own_trace:
+        copy.wait()
+    ring_wait(bands, last_in, trace_sem, 1)
+    unpack_last(last_in, bands)
     make_table(bands, rproj_ref, ltab, lside)
     for chunk in range(2):
         belongs = seg[0:1, :] == iota((ND, SEGS), 0).astype(F32)
@@ -476,9 +509,17 @@
         return carry
 
     lax.fori_loop(0, 3, band_flux, 0)
-    ring(rflux, rflux_in, back_sem, my_rows)
-    own_back = pltpu.make_async_copy(rflux.at[my_rows], rflux_in.at[my_rows], own_sem.at[6])
-    own_back.start()
+    ring_wait(faces_r, last_out, trace_sem, 0)
+    pack_last(rflux, last_out)
+
+    def send_back(p, carry):
+        ring_send(lax.rem(mi + p, NR), rflux, rflux_in, last_out, last_back, back_sem)
+        return carry
+
+    lax.fori_loop(1, NR, send_back, 0)
+    own_back = ring_own(rflux, rflux_in, last_out, last_back, 8)
+    for copy in own_back:
+        copy.start()
 
     def fields(ref, chunk, pp):
         tile = lambda r, t: ref[message_row(chunk, 2 * (2 * pp + r) + t), :]
@@ -546,8 +587,10 @@
             flux = 0.5 * y[vh * FACE : vh * FACE + FACE, :]
             add(su, 0, v, (TIME_STEP * LIFT) * (flux - mine[v]))
 
-    own_back.wait()
-    ring_wait(rflux_in, back_sem.at[1])
+    for copy in own_back:
+        copy.wait()
+    ring_wait(rflux_in, last_back, back_sem, 1)
+    unpack_last(last_back, rflux_in)
     mine = face_flux(rs, NODES - 1)
     for t in range(3):
         turned = jnp.concatenate(
@@ -560,8 +603,7 @@
 
     part = code_out.at[pl.ds(0, ND - 1)]
     pltpu.make_async_copy(part, part, code_sem.at[0]).wait()
-    ring_wait(faces_r, trace_sem.at[0])
-    ring_wait(rflux, back_sem.at[0])
+    ring_wait(rflux, last_out, back_sem, 0)
     for chunk in range(4):
         rows = rout.at[pl.ds(0, (ND - 1) * SENT)]
         pltpu.make_async_copy(rows, rows, send_sem).wait()
@@ -569,8 +611,13 @@
 
 def finish(ru, su, rnext, snext, sem):
     copies = [
-        pltpu.make_async_copy(held.at[t], out.at[:, pl.ds(t * 128, 128)], sem.at[n, t])
+        pltpu.make_async_copy(
+            held.at[t, pl.ds(v * 512, 512)],
+            out.at[pl.ds(v * 512, 512), pl.ds(t * 128, 128)],
+            sem.at[n, t, v],
+        )
         for n, (held, out) in enumerate(((ru, rnext), (su, snext)))
+        for v in range(5)
         for t in range(3)
     ]
     for copy in copies:
@@ -601,15 +648,16 @@
             V((2 * CHUNK_ROWS, 128), F32), V((2 * CHUNK_ROWS, 128), F32),
             V((2 * CHUNK_ROWS, 128), F32), V((2 * CHUNK_ROWS, 128), F32),
             V((ELEMS, 384), F32), V((ELEMS, 384), F32),
+            V((ELEMS // 2, 128), F32), V((ELEMS // 2, 128), F32), V((ELEMS // 2, 128), F32),
             V((CAP * ND, SEGS), BF16), V((SEGS, 384), F32),
-            dma((2, 3)), dma((7,)), dma((2,)), dma((2,)), dma, dma((2,)), dma((2,)), dma((2,)),
+            dma((2, 3)), dma((10,)), dma((2,)), dma((2, 2)), dma, dma((2,)), dma((2,)), dma((2, 2)),
         ],
         compiler_params=pltpu.CompilerParams(
             collective_id=0, has_side_effects=True, vmem_limit_bytes=48 * 2**20
         ),
     )(
         seg_owner.reshape(1, SEGS),
-        seg_row.reshape(1, SEGS),
+        seg_row,
         rotor_projection,
         proj_stator,
         rotor_state.reshape(state),
@@ -620,7 +668,7 @@
         out_shape=(big, big),
         in_specs=[hbm, hbm],
         out_specs=(hbm, hbm),
-        scratch_shapes=[dma((2, 3))],
+        scratch_shapes=[dma((2, 3, 5))],
         compiler_params=pltpu.CompilerParams(vmem_limit_bytes=4 * 2**20),
     )(*parts)
     return rotor_next.reshape(rotor_state.shape), stator_next.reshape(stator_state.shape)

time: 81.3 us -> 75.6 us (0.930)
  Pallas kernels: 79.1 us -> 74.7 us
  local copies, waits for them, and re-layouts: 1.27 us -> 0 us
    pallas_call x1, Pallas kernels: 75.9 us -> 71.3 us  [body(): pl.pallas_call(mega, out_shape=(V(held, F32), V(held, F32)), in_specs=[vm...]
    reshape x1 -> x0, local copies, waits for them, and re-layouts: 1.27 us -> none  [body(): seg_row.reshape(1, SEGS)]
where the time goes in v3:
time: 75.6 us; the launch traced here: 75.5 us
  Pallas kernels  74.7 us (99%)
  between operations  0.8 us (1%)
    pallas_call x1, Pallas kernels, body(): pl.pallas_call(mega, out_shape=(V(held, F32), V(held, F32)), in_specs=[vm...  71.3 us
    pallas_call x1, Pallas kernels, body(): pl.pallas_call(finish, out_shape=(big, big), in_specs=[hbm, hbm], out_spe...  3.37 us

profile of v3, /device:TPU:1, one launch (start us, length us, event | category | flops | bytes accessed | tf_op | source)
XLA Modules:
  0.0 75.5 jit_solution(5049958534059510063)
XLA Ops:
  0.6 71.3 %shard_map.77 = (f32[3,2560,128]{2,1,0:T(8,128)S(1)}, f32[3,2560,128]{2,1,0:T(8,128)S(1)}) custom-call(s32[1,768]{1,0:T(1,128)} %bitcast.7, s32[768]{0:T(1024)} %row_ref.1, f32[2,64,64]{2,1,0:T(8,128)} %rproj_ref.1, f32[2,64,64]{2,1,0:T(8,128)} %sproj_ref.1, f32[2560,384]{1,0:T(8,128)} %bitcast.5, f32[2560,384]{1,0:T(8,128)} %bitcast.6), custom_call_target="tpu_custom_call" | custom-call | tf_op jit(solution)/shard_map/pallas_call | solution.py:637
  71.9 3.4 %shard_map.78 = (f32[2560,384]{1,0:T(8,128)}, f32[2560,384]{1,0:T(8,128)}) custom-call(f32[3,2560,128]{2,1,0:T(8,128)S(1)} %get-tuple-element.6.ru, f32[3,2560,128]{2,1,0:T(8,128)S(1)} %get-tuple-element.7.su), custom_call_target="tpu_custom_call" | custom-call | tf_op jit(solution)/shard_map/pallas_call | solution.py:666

commit v4 on v3

--- a/solution.py
+++ b/solution.py
@@ -306,7 +306,7 @@
         return (lax.div(d, NS), lax.rem(d, NS))
 
     def peer(p):
-        o = lax.rem(p * 37, ND)
+        o = lax.rem(p * 53, ND)
         return lax.rem(lax.div(o, NS) + mi, NR), lax.rem(lax.rem(o, NS) + mj, NS)
 
     barrier = pltpu.get_barrier_semaphore()
@@ -391,7 +391,8 @@
         ring_send(lax.rem(mi + p, NR), faces_r, bands, last_out, last_in, trace_sem)
         return carry
 
-    lax.fori_loop(1, ND, send_code, 0)
+    for p in range(1, ND):
+        send_code(p, 0)
     lax.fori_loop(1, NR, send_trace, 0)
     own = pltpu.make_async_copy(code_out.at[me], code_in.at[me], own_sem.at[0])
     own.start()
@@ -587,11 +588,11 @@
             flux = 0.5 * y[vh * FACE : vh * FACE + FACE, :]
             add(su, 0, v, (TIME_STEP * LIFT) * (flux - mine[v]))
 
+    mine = face_flux(rs, NODES - 1)
     for copy in own_back:
         copy.wait()
     ring_wait(rflux_in, last_back, back_sem, 1)
     unpack_last(last_back, rflux_in)
-    mine = face_flux(rs, NODES - 1)
     for t in range(3):
         turned = jnp.concatenate(
             [rflux_in[g * 128 : g * 128 + 128, t * 128 : t * 128 + 128].T for g in range(3)], axis=1

time: 75.6 us -> 73.9 us (0.978)
  Pallas kernels: 74.7 us -> 73 us
    pallas_call x1, Pallas kernels: 71.3 us -> 69.6 us  [body(): pl.pallas_call(mega, out_shape=(V(held, F32), V(held, F32)), in_specs=[vm...]
where the time goes in v4:
time: 73.9 us; the launch traced here: 73.8 us
  Pallas kernels  73 us (99%)
  between operations  0.8 us (1%)
    pallas_call x1, Pallas kernels, body(): pl.pallas_call(mega, out_shape=(V(held, F32), V(held, F32)), in_specs=[vm...  69.6 us
    pallas_call x1, Pallas kernels, body(): pl.pallas_call(finish, out_shape=(big, big), in_specs=[hbm, hbm], out_spe...  3.37 us

profile of v4, /device:TPU:1, one launch (start us, length us, event | category | flops | bytes accessed | tf_op | source)
XLA Modules:
  0.0 73.8 jit_solution(7826863276636827509)
XLA Ops:
  0.6 69.6 %shard_map.77 = (f32[3,2560,128]{2,1,0:T(8,128)S(1)}, f32[3,2560,128]{2,1,0:T(8,128)S(1)}) custom-call(s32[1,768]{1,0:T(1,128)} %bitcast.7, s32[768]{0:T(1024)} %row_ref.1, f32[2,64,64]{2,1,0:T(8,128)} %rproj_ref.1, f32[2,64,64]{2,1,0:T(8,128)} %sproj_ref.1, f32[2560,384]{1,0:T(8,128)} %bitcast.5, f32[2560,384]{1,0:T(8,128)} %bitcast.6), custom_call_target="tpu_custom_call" | custom-call | tf_op jit(solution)/shard_map/pallas_call | solution.py:638
  70.3 3.4 %shard_map.78 = (f32[2560,384]{1,0:T(8,128)}, f32[2560,384]{1,0:T(8,128)}) custom-call(f32[3,2560,128]{2,1,0:T(8,128)S(1)} %get-tuple-element.6.ru, f32[3,2560,128]{2,1,0:T(8,128)S(1)} %get-tuple-element.7.su), custom_call_target="tpu_custom_call" | custom-call | tf_op jit(solution)/shard_map/pallas_call | solution.py:667

commit v5 on v4

--- a/solution.py
+++ b/solution.py
@@ -400,7 +400,7 @@
     for copy in own_trace:
         copy.start()
 
-    volume(rs, ru, prim, tmp, acc, range(2))
+    volume(rs, ru, prim, tmp, acc, range(1))
 
     own.wait()
     part = code_in.at[pl.ds(0, ND - 1)]
@@ -464,7 +464,7 @@
             seg_hots[rows, cols] = hot(slot == iota((ELEMS, ND), 1) + r * ND)
             line = code_rows[r : r + 1, :] - (1 + s * ELEMS)
             sum_hots[rows, cols] = hot(line == iota((ELEMS, ND), 0))
-    volume(rs, ru, prim, tmp, acc, range(2, 3))
+    volume(rs, ru, prim, tmp, acc, range(1, 3))
     volume(ss, su, prim, tmp, acc, range(3))
 
     lower = iota((ND, 128), 1) < FACE

time: 73.9 us -> 73.9 us (level)
  no operation moved by 1% of the time
where the time goes in v5:
time: 73.9 us; the launch traced here: 73.8 us
  Pallas kernels  73 us (99%)
  between operations  0.8 us (1%)
    pallas_call x1, Pallas kernels, body(): pl.pallas_call(mega, out_shape=(V(held, F32), V(held, F32)), in_specs=[vm...  69.6 us
    pallas_call x1, Pallas kernels, body(): pl.pallas_call(finish, out_shape=(big, big), in_specs=[hbm, hbm], out_spe...  3.37 us

profile of v5, /device:TPU:1, one launch (start us, length us, event | category | flops | bytes accessed | tf_op | source)
XLA Modules:
  0.0 73.8 jit_solution(3585420093168554269)
XLA Ops:
  0.6 69.6 %shard_map.77 = (f32[3,2560,128]{2,1,0:T(8,128)S(1)}, f32[3,2560,128]{2,1,0:T(8,128)S(1)}) custom-call(s32[1,768]{1,0:T(1,128)} %bitcast.7, s32[768]{0:T(1024)} %row_ref.1, f32[2,64,64]{2,1,0:T(8,128)} %rproj_ref.1, f32[2,64,64]{2,1,0:T(8,128)} %sproj_ref.1, f32[2560,384]{1,0:T(8,128)} %bitcast.5, f32[2560,384]{1,0:T(8,128)} %bitcast.6), custom_call_target="tpu_custom_call" | custom-call | tf_op jit(solution)/shard_map/pallas_call | solution.py:638
  70.3 3.4 %shard_map.78 = (f32[2560,384]{1,0:T(8,128)}, f32[2560,384]{1,0:T(8,128)}) custom-call(f32[3,2560,128]{2,1,0:T(8,128)S(1)} %get-tuple-element.6.ru, f32[3,2560,128]{2,1,0:T(8,128)S(1)} %get-tuple-element.7.su), custom_call_target="tpu_custom_call" | custom-call | tf_op jit(solution)/shard_map/pallas_call | solution.py:667
